TPU v7x, 128 devices: a whole 4x4x4 slice. The times are simulated.
128 devices in a mesh: rows: 16 (over z, y), cols: 8 (over x, core).
Axes of the slice: x: 4, y: 4, z: 4, core: 2. Of those that a mesh axis runs over, the one named last changes fastest.
Arguments:
- start_basis: bfloat16 [65536, 128], P('rows'), may hold values from -6 to 6
- block_values: bfloat16 [16, 8, 32, 256, 256], P('rows', 'cols'), may hold values from -0.15625 to 0.15625
- slot_count: int32 [16, 8], P('rows', 'cols'), may hold values from 1 to 32, as said below
- slot_row: int32 [16, 8, 32], P('rows', 'cols'), may hold values from 0 to 15
- slot_col: int32 [16, 8, 32], P('rows', 'cols'), may hold values from 0 to 255, as said below
Outputs:
- new_basis: float32 [65536, 128], P(('rows', 'cols'))
- triangle: float32 [128, 128], replicated
Inputs may be any that keep to these rules, and one draw needn't show every extreme that they name: `slot_count`: exactly one device in every draw holds 32 live slots. `slot_col`: on device (r, c) every slot's block column j has (j % 16) // 2 equal to c; pairs may repeat, and repeated blocks add.
All inputs are finite; a program needn't handle non-finite values.
Results may differ from a plain program's by a relative error of at most 0.0021.
Values may be sent and summed in bfloat16 or wider, within the bound.
A program may use at most 64 MiB of HBM per device.

v0:
```python
import jax
import jax.numpy as jnp
from jax import lax
from jax.sharding import PartitionSpec as P

slot_group = 16


def global_gram(matrix):
    partial_gram = jnp.dot(
        matrix.T, matrix, precision=lax.Precision.HIGHEST, preferred_element_type=jnp.float32
    )
    return lax.psum(partial_gram, ("rows", "cols"))


def upper_factor(gram):
    order = gram.shape[0]
    positions = jnp.arange(order, dtype=jnp.int32)

    def factor_step(column, carry):
        schur, upper = carry
        line = lax.dynamic_slice_in_dim(schur, column, 1, 0)[0]
        pivot_value = jnp.sqrt(jnp.sum(jnp.where(positions == column, line, 0.0)))
        scaled = jnp.where(positions >= column, line / pivot_value, 0.0)
        upper = upper + jnp.where(positions[:, None] == column, scaled[None, :], 0.0)
        schur = schur - scaled[:, None] * scaled[None, :]
        return (schur, upper)

    schur, upper = lax.fori_loop(
        0, order, factor_step, (gram, jnp.zeros((order, order), jnp.float32))
    )
    return upper


def invert_upper(upper):
    order = upper.shape[0]
    positions = jnp.arange(order, dtype=jnp.int32)

    def invert_step(count, inverse):
        which = order - 1 - count
        line = lax.dynamic_slice_in_dim(upper, which, 1, 0)[0]
        diagonal_value = jnp.sum(jnp.where(positions == which, line, 0.0))
        beyond = jnp.where(positions > which, line, 0.0)
        unit = jnp.where(positions == which, 1.0, 0.0).astype(jnp.float32)
        carried = jnp.dot(
            beyond, inverse, precision=lax.Precision.HIGHEST, preferred_element_type=jnp.float32
        )
        solved = (unit - carried) / diagonal_value
        return inverse + jnp.where(positions[:, None] == which, solved[None, :], 0.0)

    return lax.fori_loop(0, order, invert_step, jnp.zeros((order, order), jnp.float32))


def body(start_basis, block_values, slot_count, slot_row, slot_col):
    depth = start_basis.shape[1]
    width = block_values.shape[-1]
    panel_blocks = start_basis.shape[0] // width
    sub_blocks = panel_blocks // lax.axis_size("cols")
    col_index = lax.axis_index("cols")
    own_part = lax.dynamic_slice_in_dim(
        start_basis, col_index * sub_blocks * width, sub_blocks * width, 0
    )
    basis_parts = lax.all_gather(own_part, "rows", axis=0, tiled=True).reshape(-1, width, depth)
    values = block_values[0, 0]
    live_count = slot_count[0, 0]
    row_ids = slot_row[0, 0]
    col_ids = slot_col[0, 0]
    local_cols = col_ids // panel_blocks * sub_blocks + col_ids % sub_blocks
    group_total = (live_count + slot_group - 1) // slot_group

    def group_items(group_id):
        first_slot = group_id * slot_group
        tiles = lax.dynamic_slice_in_dim(values, first_slot, slot_group, 0)
        row_part = lax.dynamic_slice_in_dim(row_ids, first_slot, slot_group, 0)
        col_part = lax.dynamic_slice_in_dim(local_cols, first_slot, slot_group, 0)
        active = first_slot + jnp.arange(slot_group, dtype=jnp.int32) < live_count
        return (tiles, row_part, col_part, active)

    def forward(group_id, total):
        tiles, row_part, col_part, active = group_items(group_id)
        picked = basis_parts[col_part]
        terms = jnp.einsum("sab,sbk->sak", tiles, picked, preferred_element_type=jnp.float32)
        terms = jnp.where(active[:, None, None], terms, 0.0)
        return total.at[row_part].add(terms)

    image_part = lax.fori_loop(
        0, group_total, forward, jnp.zeros((panel_blocks, width, depth), jnp.float32)
    )
    image = lax.psum(image_part, "cols").astype(jnp.bfloat16)
    total_blocks = basis_parts.shape[0]

    def backward(group_id, total):
        tiles, row_part, col_part, active = group_items(group_id)
        inside = active & (col_part >= 0) & (col_part < total_blocks)
        picked = image[row_part]
        terms = jnp.einsum("sab,sak->sbk", tiles, picked, preferred_element_type=jnp.float32)
        terms = jnp.where(inside[:, None, None], terms, 0.0)
        return total.at[jnp.clip(col_part, 0, total_blocks - 1)].add(terms)

    back_part = lax.fori_loop(
        0, group_total, backward, jnp.zeros((total_blocks, width, depth), jnp.float32)
    )
    local_rows = lax.psum_scatter(back_part, "rows", scatter_dimension=0, tiled=True).reshape(
        -1, depth
    )
    first_upper = upper_factor(global_gram(local_rows))
    interim = jnp.dot(
        local_rows,
        invert_upper(first_upper),
        precision=lax.Precision.HIGHEST,
        preferred_element_type=jnp.float32,
    )
    second_upper = upper_factor(global_gram(interim))
    finished = jnp.dot(
        interim,
        invert_upper(second_upper),
        precision=lax.Precision.HIGHEST,
        preferred_element_type=jnp.float32,
    )
    combined = jnp.dot(
        second_upper,
        first_upper,
        precision=lax.Precision.HIGHEST,
        preferred_element_type=jnp.float32,
    )
    root = jnp.sqrt(jnp.float32(lax.axis_size("rows") * panel_blocks * width))
    return (finished * root, combined / root)


def solution(mesh):
    return jax.shard_map(
        body,
        mesh=mesh,
        in_specs=(
            P("rows", None),
            P("rows", "cols", None, None, None),
            P("rows", "cols"),
            P("rows", "cols", None),
            P("rows", "cols", None),
        ),
        out_specs=(P(("rows", "cols"), None), P()),
        check_vma=False,
    )
```

profile of v0, /device:TPU:1, one launch (start us, length us, event | category | flops | bytes accessed | tf_op | source)
XLA Modules:
  0.0 2184.8 jit_solution(14717494994902630408)
XLA Ops:
  9.8 6.4 copy.7
  16.3 42.0 %all-gather.2.cloned.1.call-done = bf16[8192,128]{1,0:T(8,128)(2,1)} async-done(((bf16[512,128]{1,0:T(8,128)(2,1)}), bf16[8192,128]{1,0:T(8,128)(2,1)}) %all-gather.2.cloned.1.call-update) | async-done | bytes 2097168 | tf_op jit(solution)/shard_map/all_gather | solution.py:63
  58.2 1.6 broadcast_in_dim.287
  59.8 11.0 while.88
  59.9 3.3 gather_fusion
  63.9 2.6 fusion.83
  66.4 4.3 scatter_fusion
  70.7 53.6 %all-reduce.7 = bf16[16,256,128]{2,1,0:T(8,128)(2,1)} all-reduce(f32[16,256,128]{2,1,0:T(8,128)} %get-tuple-element.478), channel_id=1, replica_groups=mesh['rows'=16,'cols'=8] {'cols'}, use_global_device_ids=true, to_apply=%region_3.4 | all-reduce | flops 524288 | bytes 3145728 | tf_op jit(solution)/shard_map/psum | solution.py:89
  124.4 2.5 broadcast_in_dim.286
  126.8 10.6 while.89
  127.6 2.9 gather_fusion.1
  130.5 2.5 fusion.86
  133.1 4.4 scatter_fusion.1
  137.6 87.8 %reduce-scatter.2.cloned.1.call-done = f32[2,256,128]{2,1,0:T(8,128)} async-done(((f32[32,256,128]{2,1,0:T(8,128)}), f32[2,256,128]{2,1,0:T(8,128)}) %reduce-scatter.2.cloned.1.call-update) | async-done | bytes 262160 | tf_op jit(solution)/shard_map/reduce_scatter | solution.py:103
  225.3 2.3 convolution_bitcast_fusion.2
  227.8 142.4 %all-reduce.4.cloned.1.call-done = f32[128,128]{1,0:T(8,128)} async-done(((f32[128,128]{1,0:T(8,128)}), f32[128,128]{1,0:T(8,128)}) %all-reduce.4.cloned.1.call-update) | async-done | bytes 65552 | tf_op jit(solution)/shard_map/psum | solution.py:13
  370.1 628.4 %while.90 = (s32[]{:T(128)}, f32[128,128]{1,0:T(8,128)}, f32[128,128]{1,0:T(8,128)S(1)}, s32[]{:T(128)}, s32[]{:T(128)}) while((s32[]{:T(128)}, f32[128,128]{1,0:T(8,128)}, f32[128,128]{1,0:T(8,128)S(1)}, s32[]{:T(128)}, s32[]{:T(128)}) %tuple.190), condition=%wide.region_11.12_spmd.clone.clone, body=%wide.region_9.11_spmd.clone.clone.sunk | while | flops 83202 | bytes 269151 | solution.py:29
  998.5 198.6 %while.91 = (s32[]{:T(128)}, f32[128,128]{1,0:T(8,128)S(1)}, f32[128,128]{1,0:T(8,128)S(1)}, s32[]{:T(128)}, s32[]{:T(128)}, /*index=5*/s32[]{:T(128)}, s32[]{:T(128)}) while((s32[]{:T(128)}, f32[128,128]{1,0:T(8,128)S(1)}, f32[128,128]{1,0:T(8,128)S(1)}, s32[]{:T(128)}, s32[]{:T(128)}, /*index=5*/s32[]{:T(128)}, ...), condition=%wide.region_14.15_spmd.clone.clone, body=%wide.region_12.14_spmd.clone.clone.sunk | while | flops 263430 | bytes 201113 | solution.py:51
  1198.8 134.8 %all-reduce.6.cloned.1.call-done = f32[128,128]{1,0:T(8,128)} async-done(((f32[128,128]{1,0:T(8,128)}), f32[128,128]{1,0:T(8,128)}) %all-reduce.6.cloned.1.call-update) | async-done | bytes 65552 | tf_op jit(solution)/shard_map/psum | solution.py:13
  1333.6 628.4 %while.92 = (s32[]{:T(128)}, f32[128,128]{1,0:T(8,128)}, f32[128,128]{1,0:T(8,128)S(1)}, s32[]{:T(128)}, s32[]{:T(128)}) while((s32[]{:T(128)}, f32[128,128]{1,0:T(8,128)}, f32[128,128]{1,0:T(8,128)S(1)}, s32[]{:T(128)}, s32[]{:T(128)}) %tuple.196), condition=%wide.region_18.19_spmd.clone.clone, body=%wide.region_16.18_spmd.clone.clone.sunk | while | flops 83202 | bytes 269151 | solution.py:29
  1337.0 1.5 select_add_fusion.10
  1341.9 1.5 select_add_fusion.10
  1346.8 1.5 select_add_fusion.10
  1351.7 1.5 select_add_fusion.10
  1356.6 1.5 select_add_fusion.10
  1361.6 1.5 select_add_fusion.10
  1366.5 1.5 select_add_fusion.10
  1371.4 1.5 select_add_fusion.10
  1381.3 1.5 select_add_fusion.10
  1391.1 1.5 select_add_fusion.10
  1396.0 1.5 select_add_fusion.10
  1401.0 1.5 select_add_fusion.10
  1405.9 1.5 select_add_fusion.10
  1415.7 1.5 select_add_fusion.10
  1420.6 1.5 select_add_fusion.10
  1425.5 1.5 select_add_fusion.10
  1435.3 1.5 select_add_fusion.10
  1440.2 1.5 select_add_fusion.10
  1445.1 1.5 select_add_fusion.10
  1454.9 1.5 select_add_fusion.10
  1464.7 1.5 select_add_fusion.10
  1469.6 1.5 select_add_fusion.10
  1474.5 1.5 select_add_fusion.10
  1479.4 1.5 select_add_fusion.10
  1489.2 1.5 select_add_fusion.10
  1499.0 1.5 select_add_fusion.10
  1503.9 1.5 select_add_fusion.10
  1962.8 214.4 %while.93 = (s32[]{:T(128)}, f32[128,128]{1,0:T(8,128)S(1)}, f32[128,128]{1,0:T(8,128)S(1)}, s32[]{:T(128)}, s32[]{:T(128)}, /*index=5*/s32[]{:T(128)}, s32[]{:T(128)}) while((s32[]{:T(128)}, f32[128,128]{1,0:T(8,128)S(1)}, f32[128,128]{1,0:T(8,128)S(1)}, s32[]{:T(128)}, s32[]{:T(128)}, /*index=5*/s32[]{:T(128)}, ...), condition=%wide.region_21.22_spmd.clone.clone, body=%wide.region_19.21_spmd.clone.clone.sunk | while | flops 263430 | bytes 201113 | solution.py:51
  (2309 shorter events, 1447.2 us)
Async XLA Ops:
  7.2 1.2 copy-start
  7.2 51.0 %all-gather.2.cloned.1.call-start = ((), (), s32[]{:S(2)}) async-start(), calls=%async_computation.1 | async-start | bytes 2228224 | tf_op jit(solution)/shard_map/all_gather | solution.py:63
  9.1 216.3 %reduce-scatter.2.cloned.1.call-start = ((), (), s32[]{:S(2)}) async-start(), calls=%async_computation.2 | async-start | bytes 4456448 | tf_op jit(solution)/shard_map/reduce_scatter | solution.py:103
  9.8 6.4 copy-start.3
  16.2 43.6 %copy-start.2 = (s32[1,1,32]{2,1,0:T(1,128)S(1)}, s32[1,1,32]{2,1,0:T(1,128)}, u32[]{:S(2)}) copy-start(s32[1,1,32]{2,1,0:T(1,128)} %param.20) | copy-start | bytes 388
  137.5 232.6 %all-reduce.4.cloned.1.call-start = ((), (), s32[]{:S(2)}) async-start(), calls=%async_computation.3 | async-start | bytes 131072 | tf_op jit(solution)/shard_map/psum | solution.py:13
  225.3 971.8 %copy-start.1 = (f32[2,256,128]{2,1,0:T(8,128)S(1)}, f32[2,256,128]{2,1,0:T(8,128)}, u32[]{:S(2)}) copy-start(f32[2,256,128]{2,1,0:T(8,128)} %reduce-scatter.2.cloned.1.call-done) | copy-start | bytes 786436
  227.7 1105.9 %all-reduce.6.cloned.1.call-start = ((), (), s32[]{:S(2)}) async-start(), calls=%async_computation.4 | async-start | bytes 131072 | tf_op jit(solution)/shard_map/psum | solution.py:13
Sparse Core Ops, SparseCore 0:
  10.7 47.4 all-gather.1
  137.6 87.6 reduce-scatter.1
  231.4 138.7 all-reduce.3
  1198.9 134.6 all-reduce.5
where the time goes:
time: 2230 us; the launch traced here: 2180 us
  other arithmetic  1280 us (57%)
  waiting for transfers between devices  407 us (18%)
  matrix products  221 us (10%)
  loops' own time  188 us (8%)
  blocking collectives  53.6 us (2%)
    add x256, other arithmetic, factor_step(): upper + jnp.where(positions[:, None] == column, scaled[None, :], 0.0)  396 us
    reduce_sum x256, other arithmetic, factor_step(): pivot_value = jnp.sqrt(jnp.sum(jnp.where(positions == column, line, 0.0)))  329 us
    psum x2, waiting for transfers between devices, global_gram(): return lax.psum(partial_gram, ('rows', 'cols'))  277 us
    dot_general x256, matrix products, invert_step(): jnp.dot(beyond, inverse, precision=lax.Precision.HIGHEST, preferred_eleme...  210 us
    another operation x2, loops' own time, upper_factor(): lax.fori_loop(0, order, factor_step, (gram, jnp.zeros((order, order), jnp...  178 us
    select_n x256, other arithmetic, factor_step(): scaled = jnp.where(positions >= column, line / pivot_value, 0.0)  177 us
    mul x256, other arithmetic, factor_step(): schur = schur - scaled[:, None] * scaled[None, :]  176 us
    reduce_sum x256, other arithmetic, invert_step(): diagonal_value = jnp.sum(jnp.where(positions == which, line, 0.0))  166 us
  transfers between devices with their start and end apart: 4, of which 4 were waited for; matrix products, arithmetic and copies ran while one was open for 0% of the time, Pallas kernels for 0%

commit v1 on v0

v1 whole, which is shorter than its diff:
```python
import functools

import jax
import jax.numpy as jnp
from jax import lax
from jax.experimental import pallas as pl
from jax.experimental.pallas import tpu as pltpu
from jax.sharding import PartitionSpec as P

SUB = 8
VMEM = pl.BlockSpec(memory_space=pltpu.VMEM)
SMEM = pl.BlockSpec(memory_space=pltpu.SMEM)
ANY = pl.BlockSpec(memory_space=pl.ANY)
NT = (((1,), (1,)), ((), ()))


def matmul(a, b, dims):
    return lax.dot_general(
        a, b, dims, precision=lax.Precision.HIGHEST, preferred_element_type=jnp.float32
    )


def fetch_live(count, values, tiles, sems):
    def start(slot, carry):
        pltpu.make_async_copy(values.at[slot], tiles.at[slot], sems.at[slot]).start()
        return carry

    lax.fori_loop(0, count, start, 0)


def forward_kernel(count_ref, row_ref, col_ref, basis, values, out, tiles, sems):
    count = count_ref[0]
    fetch_live(count, values, tiles, sems)
    out[...] = jnp.zeros_like(out)

    def step(slot, carry):
        pltpu.make_async_copy(values.at[slot], tiles.at[slot], sems.at[slot]).wait()
        term = jnp.dot(tiles[slot], basis[col_ref[slot]], preferred_element_type=jnp.float32)
        out[row_ref[slot]] += term
        return carry

    lax.fori_loop(0, count, step, 0)


def backward_kernel(count_ref, row_ref, col_ref, image, values, out, tiles, flipped, sems):
    count = count_ref[0]
    fetch_live(count, values, tiles, sems)
    out[...] = jnp.zeros_like(out)

    def flip(row, carry):
        flipped[row] = image[row].T
        return carry

    lax.fori_loop(0, image.shape[0], flip, 0)

    def step(slot, carry):
        pltpu.make_async_copy(values.at[slot], tiles.at[slot], sems.at[slot]).wait()
        term = jnp.dot(flipped[row_ref[slot]], tiles[slot], preferred_element_type=jnp.float32)
        out[col_ref[slot]] += term
        return carry

    lax.fori_loop(0, count, step, 0)


def forward(count, rows, cols, basis, values, panel_blocks):
    slots, width, _ = values.shape
    depth = basis.shape[2]
    return pl.pallas_call(
        forward_kernel,
        out_shape=jax.ShapeDtypeStruct((panel_blocks, width, depth), jnp.float32),
        in_specs=[SMEM, SMEM, SMEM, VMEM, ANY],
        out_specs=VMEM,
        scratch_shapes=[
            pltpu.VMEM((slots, width, width), values.dtype),
            pltpu.SemaphoreType.DMA((slots,)),
        ],
        compiler_params=pltpu.CompilerParams(vmem_limit_bytes=32 << 20),
    )(count, rows, cols, basis, values)


def backward(count, rows, cols, image, values, total_blocks):
    slots, width, _ = values.shape
    panel_blocks, _, depth = image.shape
    return pl.pallas_call(
        backward_kernel,
        out_shape=jax.ShapeDtypeStruct((total_blocks, depth, width), jnp.float32),
        in_specs=[SMEM, SMEM, SMEM, VMEM, ANY],
        out_specs=VMEM,
        scratch_shapes=[
            pltpu.VMEM((slots, width, width), values.dtype),
            pltpu.VMEM((panel_blocks, depth, width), image.dtype),
            pltpu.SemaphoreType.DMA((slots,)),
        ],
        compiler_params=pltpu.CompilerParams(vmem_limit_bytes=32 << 20),
    )(count, rows, cols, image, values)


def factor(gram, upper_ref, inverse_ref):
    order = gram.shape[0]
    lead = gram
    tail = (
        lax.broadcasted_iota(jnp.int32, (order, order), 0)
        == lax.broadcasted_iota(jnp.int32, (order, order), 1)
    ).astype(jnp.float32)
    for base in range(0, order, SUB):
        left = order - base
        columns = [
            jnp.broadcast_to(lead[:, base + k : base + k + 1], (left, order)) for k in range(SUB)
        ]
        position = lax.broadcasted_iota(jnp.int32, (left, order), 0)
        top = lax.broadcasted_iota(jnp.int32, (SUB, order), 0)
        lane = lax.broadcasted_iota(jnp.int32, (SUB, order), 1)
        pivots = jnp.zeros((SUB, order), jnp.float32)
        for k in range(SUB):
            pivot = columns[k][k : k + 1, :]
            pivots = jnp.where(top == k, pivot, pivots)
            ratio = jnp.where(position > k, columns[k] * (1.0 / pivot), 0.0)
            lead = lead - ratio * lead[k : k + 1, :]
            tail = tail - ratio * tail[k : k + 1, :]
            for j in range(k + 1, SUB):
                columns[j] = columns[j] - ratio * columns[j][k : k + 1, :]
        scale = 1.0 / jnp.sqrt(pivots)
        upper_ref[base : base + SUB, :] = jnp.where(lane >= base + top, lead[:SUB] * scale, 0.0)
        inverse_ref[base : base + SUB, :] = tail[:SUB] * scale
        lead = lead[SUB:]
        tail = tail[SUB:]


def first_kernel(gram_ref, x_ref, upper_ref, q_ref, part_ref, inverse):
    factor(gram_ref[...], upper_ref, inverse)
    for s in range(x_ref.shape[0]):
        q_ref[s] = matmul(inverse[...], x_ref[s], (((1,), (0,)), ((), ())))
    part_ref[...] = matmul(q_ref[0], q_ref[0], NT)
    for s in range(1, x_ref.shape[0]):
        part_ref[...] += matmul(q_ref[s], q_ref[s], NT)


def last_kernel(root, gram_ref, upper_ref, q_ref, basis_ref, triangle_ref, second, inverse):
    factor(gram_ref[...], second, inverse)
    width = q_ref.shape[2]
    for s in range(q_ref.shape[0]):
        done = matmul(inverse[...], q_ref[s], (((1,), (0,)), ((), ())))
        basis_ref[s * width : (s + 1) * width, :] = done.T * root
    triangle_ref[...] = matmul(second[...], upper_ref[...], (((1,), (0,)), ((), ()))) / root


def gram_kernel(x_ref, part_ref):
    part_ref[...] = matmul(x_ref[0], x_ref[0], NT)
    for s in range(1, x_ref.shape[0]):
        part_ref[...] += matmul(x_ref[s], x_ref[s], NT)


def body(start_basis, block_values, slot_count, slot_row, slot_col):
    depth = start_basis.shape[1]
    width = block_values.shape[-1]
    panel_blocks = start_basis.shape[0] // width
    sub_blocks = panel_blocks // lax.axis_size("cols")
    col_index = lax.axis_index("cols")
    own_part = lax.dynamic_slice_in_dim(
        start_basis, col_index * sub_blocks * width, sub_blocks * width, 0
    )
    basis_parts = lax.all_gather(own_part, "rows", axis=0, tiled=True).reshape(-1, width, depth)
    values = block_values[0, 0]
    count = slot_count[0]
    row_ids = slot_row[0, 0]
    col_ids = slot_col[0, 0]
    local_cols = col_ids // panel_blocks * sub_blocks + col_ids % sub_blocks
    image_part = forward(count, row_ids, local_cols, basis_parts, values, panel_blocks)
    image = lax.psum(image_part, "cols").astype(jnp.bfloat16)
    back_part = backward(count, row_ids, local_cols, image, values, basis_parts.shape[0])
    mine = lax.psum_scatter(back_part, "rows", scatter_dimension=0, tiled=True)

    square = jax.ShapeDtypeStruct((depth, depth), jnp.float32)
    room = pltpu.VMEM((depth, depth), jnp.float32)
    part = pl.pallas_call(gram_kernel, out_shape=square, in_specs=[VMEM], out_specs=VMEM)(mine)
    gram = lax.psum(part, ("rows", "cols"))
    upper, interim, part = pl.pallas_call(
        first_kernel,
        out_shape=[square, jax.ShapeDtypeStruct(mine.shape, jnp.float32), square],
        in_specs=[VMEM] * 2,
        out_specs=[VMEM] * 3,
        scratch_shapes=[room],
    )(gram, mine)
    gram = lax.psum(part, ("rows", "cols"))
    root = float(lax.axis_size("rows") * panel_blocks * width) ** 0.5
    return pl.pallas_call(
        functools.partial(last_kernel, root),
        out_shape=[jax.ShapeDtypeStruct((sub_blocks * width, depth), jnp.float32), square],
        in_specs=[VMEM] * 3,
        out_specs=[VMEM] * 2,
        scratch_shapes=[room, room],
    )(gram, upper, interim)


def solution(mesh):
    return jax.shard_map(
        body,
        mesh=mesh,
        in_specs=(
            P("rows", None),
            P("rows", "cols", None, None, None),
            P("rows", "cols"),
            P("rows", "cols", None),
            P("rows", "cols", None),
        ),
        out_specs=(P(("rows", "cols"), None), P()),
        check_vma=False,
    )
```

time: 2230 us -> 513 us (0.23); the launches traced: 2180 us -> 513 us
  other arithmetic: 1280 us -> 0.67 us
  matrix products: 221 us -> 0 us
  loops' own time: 188 us -> 0 us
  Pallas kernels: 0 us -> 28.2 us
    reduce_sum x512 -> x0, other arithmetic: 495 us -> none  [the longest x256 329 us: factor_step(): pivot_value = jnp.sqrt(jnp.sum(jnp.where(positions == column, line, 0.0)))]
    add x512 -> x0, other arithmetic: 419 us -> none  [the longest x256 396 us: factor_step(): upper + jnp.where(positions[:, None] == column, scaled[None, :], 0.0)]
    dot_general x263 -> x0, matrix products: 221 us -> none  [the longest x256 210 us: invert_step(): jnp.dot(beyond, inverse, precision=lax.Precision.HIGHEST, preferred_eleme...]
    another operation x6 -> x0, loops' own time: 188 us -> none  [the longest x2 178 us: upper_factor(): lax.fori_loop(0, order, factor_step, (gram, jnp.zeros((order, order), jnp...]
    select_n x258 -> x0, other arithmetic: 177 us -> none  [the longest x256 177 us: factor_step(): scaled = jnp.where(positions >= column, line / pivot_value, 0.0)]
    mul x256 -> x0, other arithmetic: 176 us -> none  [factor_step(): schur = schur - scaled[:, None] * scaled[None, :]]
    pallas_call x0 -> x5, Pallas kernels: none -> 28.2 us  [the longest x1 7.37 us: backward(): pl.pallas_call(backward_kernel, out_shape=jax.ShapeDtypeStruct((total_blo...]
where the time goes in v1:
time: 513 us
  waiting for transfers between devices  407 us (79%)
  blocking collectives  51.1 us (10%)
  Pallas kernels  28.2 us (5%)
  between operations  14.5 us (3%)
  local copies, waits for them, and re-layouts  11.6 us (2%)
    psum x2, waiting for transfers between devices, body(): gram = lax.psum(part, ('rows', 'cols'))  277 us
    reduce_scatter x1, waiting for transfers between devices, body(): mine = lax.psum_scatter(back_part, 'rows', scatter_dimension=0, tiled=True)  81.5 us
    psum x1, blocking collectives, body(): image = lax.psum(image_part, 'cols').astype(jnp.bfloat16)  51.1 us
    all_gather x1, waiting for transfers between devices, body(): lax.all_gather(own_part, 'rows', axis=0, tiled=True)  47.8 us
    unnamed x16, local copies, waits for them, and re-layouts  11 us
  transfers between devices with their start and end apart: 4, of which 4 were waited for; matrix products, arithmetic and copies ran while one was open for 0% of the time, Pallas kernels for 0%

profile of v1, /device:TPU:1, one launch (start us, length us, event | category | flops | bytes accessed | tf_op | source)
XLA Modules:
  0.0 513.0 jit_solution(15476413824625602932)
XLA Ops:
  7.2 0.0 copy-start
  7.2 0.0 all-gather.2.cloned.1.call-start
  7.2 1.2 copy-done
  8.4 0.7 constant_dynamic-slice_fusion
  9.1 0.0 all-gather.2.cloned.1.call-update
  9.1 0.0 reduce-scatter.2.cloned.1.call-start
  9.8 0.7 fusion.col_ref
  10.4 47.8 %all-gather.2.cloned.1.call-done = bf16[8192,128]{1,0:T(8,128)(2,1)} async-done(((bf16[512,128]{1,0:T(8,128)(2,1)}), bf16[8192,128]{1,0:T(8,128)(2,1)}) %all-gather.2.cloned.1.call-update) | async-done | bytes 2097168 | tf_op jit(solution)/shard_map/all_gather | solution.py:162
  58.2 0.0 copy-start.1
  58.2 2.2 copy-done.1
  60.4 0.0 copy-start.5
  60.4 1.6 copy-done.5
  62.0 0.0 copy-start.6
  62.0 0.7 copy-done.6
  62.7 0.0 copy-start.7
  62.7 6.2 %shard_map.68 = f32[16,256,128]{2,1,0:T(8,128)S(1)} custom-call(s32[1]{0:T(128)} %bitcast.15.count_ref, s32[32]{0:T(128)S(1)} %bitcast.20, s32[32]{0:T(128)S(1)} %fusion.col_ref, bf16[32,256,128]{2,1,0:T(8,128)(2,1)S(1)} %bitcast.19, bf16[32,256,256]{2,1,0:T(8,128)(2,1)S(1)} %bitcast.17), custom_call_target="tpu_custom_call" | custom-call | tf_op jit(solution)/shard_map/pallas_call | solution.py:68
  68.9 51.1 %all-reduce.7.image = bf16[16,256,128]{2,1,0:T(8,128)(2,1)} all-reduce(f32[16,256,128]{2,1,0:T(8,128)S(1)} %shard_map.68), channel_id=1, replica_groups=mesh['rows'=16,'cols'=8] {'cols'}, use_global_device_ids=true, to_apply=%region_0.1 | all-reduce | flops 524288 | bytes 3145728 | tf_op jit(solution)/shard_map/psum | solution.py:169
  120.0 0.0 copy-done.7
  120.0 0.0 copy-start.2
  120.0 2.2 copy-done.2
  122.2 0.0 copy-start.4
  122.2 1.2 copy-done.4
  123.4 7.4 %shard_map.69 = f32[32,128,256]{2,1,0:T(8,128)S(1)} custom-call(s32[1]{0:T(128)} %bitcast.16.count_ref, s32[32]{0:T(128)S(1)} %bitcast.21, s32[32]{0:T(128)S(1)} %fusion.col_ref, bf16[16,256,128]{2,1,0:T(8,128)(2,1)S(1)} %copy-done.4, bf16[32,256,256]{2,1,0:T(8,128)(2,1)S(1)} %bitcast.18), custom_call_target="tpu_custom_call" | custom-call | tf_op jit(solution)/shard_map/pallas_call | solution.py:84
  130.8 0.0 copy-start.3
  130.8 1.9 copy-done.3
  132.7 0.0 reduce-scatter.2.cloned.1.call-update
  132.8 0.0 all-reduce.4.cloned.1.call-start
  132.8 81.5 %reduce-scatter.2.cloned.1.call-done.x_ref = f32[2,128,256]{2,1,0:T(8,128)} async-done(((f32[32,128,256]{2,1,0:T(8,128)}), f32[2,128,256]{2,1,0:T(8,128)}) %reduce-scatter.2.cloned.1.call-update) | async-done | bytes 262160 | tf_op jit(solution)/shard_map/reduce_scatter | solution.py:171
  214.3 2.0 shard_map.70
  216.3 0.0 all-reduce.4.cloned.1.call-update
  216.3 0.0 all-reduce.6.cloned.1.call-start
  216.4 142.6 %all-reduce.4.cloned.1.call-done.gram_ref = f32[128,128]{1,0:T(8,128)} async-done(((f32[128,128]{1,0:T(8,128)}), f32[128,128]{1,0:T(8,128)}) %all-reduce.4.cloned.1.call-update) | async-done | bytes 65552 | tf_op jit(solution)/shard_map/psum | solution.py:176
  359.0 6.5 %shard_map.71 = (f32[128,128]{1,0:T(8,128)}, f32[2,128,256]{2,1,0:T(8,128)}, f32[128,128]{1,0:T(8,128)}) custom-call(f32[128,128]{1,0:T(8,128)} %all-reduce.4.cloned.1.call-done.gram_ref, f32[2,128,256]{2,1,0:T(8,128)} %reduce-scatter.2.cloned.1.call-done.x_ref), custom_call_target="tpu_custom_call" | custom-call | tf_op jit(solution)/shard_map/pallas_call | solution.py:177
  365.5 0.0 all-reduce.6.cloned.1.call-update
  365.6 134.8 %all-reduce.6.cloned.1.call-done.gram_ref = f32[128,128]{1,0:T(8,128)} async-done(((f32[128,128]{1,0:T(8,128)}), f32[128,128]{1,0:T(8,128)}) %all-reduce.6.cloned.1.call-update) | async-done | bytes 65552 | tf_op jit(solution)/shard_map/psum | solution.py:184
  500.3 6.1 %shard_map.72 = (f32[512,128]{1,0:T(8,128)}, f32[128,128]{1,0:T(8,128)}) custom-call(f32[128,128]{1,0:T(8,128)} %all-reduce.6.cloned.1.call-done.gram_ref, f32[128,128]{1,0:T(8,128)} %get-tuple-element.6.upper_ref, f32[2,128,256]{2,1,0:T(8,128)} %get-tuple-element.7.q_ref), custom_call_target="tpu_custom_call" | custom-call | tf_op jit(solution)/shard_map/pallas_call | solution.py:186
Async XLA Ops:
  7.2 1.2 copy-start
  7.2 51.0 %all-gather.2.cloned.1.call-start = ((), (), s32[]{:S(2)}) async-start(), calls=%async_computation.1 | async-start | bytes 2228224 | tf_op jit(solution)/shard_map/all_gather | solution.py:162
  9.1 205.2 %reduce-scatter.2.cloned.1.call-start = ((), (), s32[]{:S(2)}) async-start(), calls=%async_computation.2 | async-start | bytes 4456448 | tf_op jit(solution)/shard_map/reduce_scatter | solution.py:171
  58.2 2.2 copy-start.1
  60.4 1.6 copy-start.5
  62.0 0.7 copy-start.6
  62.7 57.3 %copy-start.7 = (s32[1,1,32]{2,1,0:T(1,128)S(1)}, s32[1,1,32]{2,1,0:T(1,128)}, u32[]{:S(2)}) copy-start(s32[1,1,32]{2,1,0:T(1,128)} %param.8) | copy-start | bytes 388
  120.0 2.2 copy-start.2
  122.2 1.2 copy-start.4
  130.8 1.9 copy-start.3
  132.8 226.2 %all-reduce.4.cloned.1.call-start = ((), (), s32[]{:S(2)}) async-start(), calls=%async_computation.3 | async-start | bytes 131072 | tf_op jit(solution)/shard_map/psum | solution.py:176
  216.3 284.0 %all-reduce.6.cloned.1.call-start = ((), (), s32[]{:S(2)}) async-start(), calls=%async_computation.4 | async-start | bytes 131072 | tf_op jit(solution)/shard_map/psum | solution.py:184
Sparse Core Ops, SparseCore 0:
  10.7 47.4 all-gather.1
  132.9 81.3 reduce-scatter.1
  220.4 138.5 all-reduce.3
  365.7 134.6 all-reduce.5

commit v2 on v1

v2 whole, which is shorter than its diff:
```python
import functools

import jax
import jax.numpy as jnp
from jax import lax
from jax.experimental import pallas as pl
from jax.experimental.pallas import tpu as pltpu
from jax.sharding import PartitionSpec as P

SUB = 8
RING = 4
VMEM = pl.BlockSpec(memory_space=pltpu.VMEM)
SMEM = pl.BlockSpec(memory_space=pltpu.SMEM)
ANY = pl.BlockSpec(memory_space=pl.ANY)
NN = (((1,), (0,)), ((), ()))
NT = (((1,), (1,)), ((), ()))


def matmul(a, b, dims):
    return lax.dot_general(
        a, b, dims, precision=lax.Precision.HIGHEST, preferred_element_type=jnp.float32
    )


class Wires:
    def __init__(self, send, recv):
        self.send, self.recv, self.used = send, recv, []

    def start(self, src, dst, device):
        at = len(self.used)
        copy = pltpu.make_async_remote_copy(
            src_ref=src,
            dst_ref=dst,
            send_sem=self.send.at[at],
            recv_sem=self.recv.at[at],
            device_id=device,
            device_id_type=pl.DeviceIdType.MESH,
        )
        copy.start()
        self.used.append(copy)
        return copy

    def drain(self):
        for copy in self.used:
            copy.wait_send()


def greet(peers):
    barrier = pltpu.get_barrier_semaphore()
    for peer in peers:
        pl.semaphore_signal(
            barrier, inc=1, device_id=peer, device_id_type=pl.DeviceIdType.MESH
        )
    pl.semaphore_wait(barrier, len(peers))


def shifted(at, offset):
    return lax.rem(at + offset % RING, RING)


class Plane:
    def __init__(self):
        row = lax.axis_index("rows")
        self.col = lax.axis_index("cols")
        self.z, self.y = row // RING, lax.rem(row, RING)

    def row(self, half, first, second):
        along_y, along_z = (first, second) if half == 0 else (second, first)
        return shifted(self.z, along_z) * RING + shifted(self.y, along_y)

    def device(self, half, first, second):
        return (self.row(half, first, second), self.col)

    def neighbours(self):
        return [self.device(0, 1, 0), self.device(0, 3, 0), self.device(0, 0, 1), self.device(0, 0, 3)]


GATHER_COPIES = 40


def gather_kernel(own, out, send, recv, local):
    plane = Plane()
    wires = Wires(send, recv)
    me = plane.row(0, 0, 0)
    keep = pltpu.make_async_copy(own, out.at[me], local)
    keep.start()
    greet(plane.neighbours())
    cut = own.shape[1] // 2
    upper, lower = pl.ds(0, cut), pl.ds(cut, cut)

    def both_ways(half, first, axis, src):
        dst = out.at[plane.row(half, first, 0), half]
        if axis == 0:
            return [wires.start(src, dst, plane.device(half, s, 0)) for s in (1, 3)]
        return [wires.start(src, dst, plane.device(half, 0, s)) for s in (1, 3)]

    along_first = [both_ways(h, 0, 0, own.at[h]) for h in (0, 1)]
    along_second = {(h, 0): both_ways(h, 0, 1, own.at[h]) for h in (0, 1)}
    relays = []
    for h in (0, 1):
        pair = []
        for at, (come_from, part, onward) in enumerate(((3, upper, 1), (1, lower, 3))):
            along_first[h][at].wait_recv()
            piece = out.at[plane.row(h, come_from, 0), h, part]
            pair.append(wires.start(piece, piece, plane.device(h, onward, 0)))
        relays.append(pair)
    for h in (0, 1):
        for f in (3, 1):
            along_second[h, f] = both_ways(h, f, 1, out.at[plane.row(h, f, 0), h])
    last = []

    def pass_on(h, f):
        for at, (come_from, part, onward) in enumerate(((3, upper, 1), (1, lower, 3))):
            along_second[h, f][at].wait_recv()
            piece = out.at[plane.row(h, f, come_from), h, part]
            last.append(wires.start(piece, piece, plane.device(h, 0, onward)))

    for h in (0, 1):
        pass_on(h, 0)
    for h in (0, 1):
        for copy in relays[h]:
            copy.wait_recv()
        along_second[h, 2] = both_ways(h, 2, 1, out.at[plane.row(h, 2, 0), h])
    for f in (3, 1, 2):
        for h in (0, 1):
            pass_on(h, f)
    for copy in last:
        copy.wait_recv()
    keep.wait()
    wires.drain()


def gather(own, rows):
    return pl.pallas_call(
        gather_kernel,
        out_shape=jax.ShapeDtypeStruct((rows,) + own.shape, own.dtype),
        in_specs=[VMEM],
        out_specs=VMEM,
        scratch_shapes=[
            pltpu.SemaphoreType.DMA((GATHER_COPIES,)),
            pltpu.SemaphoreType.DMA((GATHER_COPIES,)),
            pltpu.SemaphoreType.DMA,
        ],
        compiler_params=pltpu.CompilerParams(
            collective_id=0, has_side_effects=True, vmem_limit_bytes=32 << 20
        ),
    )(own)


IMAGE_COPIES = 24


def image_kernel(part, image, sibling, total, relayed, merged, final, send, recv):
    row, col = lax.axis_index("rows"), lax.axis_index("cols")
    x, core = col // 2, lax.rem(col, 2)
    twin = (row, x * 2 + 1 - core)
    right, left = ((row, shifted(x, s) * 2 + core) for s in (1, 3))
    wires = Wires(send, recv)
    greet([twin, right, left])
    sub = image.shape[0] // 8

    def chunk(offset, which):
        return pl.ds((shifted(x, offset) * 2 + which) * sub, sub)

    order = (2, 1, 3, 0)
    swap = {
        o: wires.start(part.at[chunk(o, 1 - core)], sibling.at[o], twin) for o in order
    }
    for o in order:
        swap[o].wait_recv()
        total[o] = part[chunk(o, core)] + sibling[o]
        if o == 2:
            up = wires.start(total.at[2, 0], relayed.at[0], right)
            down = wires.start(total.at[2, 1], relayed.at[1], left)
        elif o == 1:
            right_plain = wires.start(total.at[1, 1], final.at[0, 1], right)
        elif o == 3:
            left_plain = wires.start(total.at[3, 0], final.at[1, 0], left)
    up.wait_recv()
    merged[0] = total[1, 0] + relayed[0]
    right_sum = wires.start(merged.at[0], final.at[0, 0], right)
    down.wait_recv()
    merged[1] = total[3, 1] + relayed[1]
    left_sum = wires.start(merged.at[1], final.at[1, 1], left)

    mine = (x * 2 + core) * sub
    left_plain.wait_recv()
    right_sum.wait_recv()
    image[mine] = (total[0, 0] + (final[0, 0] + final[1, 0])).T.astype(image.dtype)
    sends = []
    for b in range(2):
        if b == 1:
            right_plain.wait_recv()
            left_sum.wait_recv()
            image[mine + 1] = (total[0, 1] + (final[0, 1] + final[1, 1])).T.astype(image.dtype)
        block = image.at[mine + b]
        sends.append([wires.start(block, block, peer) for peer in (right, left, twin)])
    hops = []
    for o, at, b_on, onward in ((3, 0, 0, right), (1, 1, 1, left)):
        start = (shifted(x, o) * 2 + core) * sub
        for b in (0, 1):
            sends[b][at].wait_recv()
            block = image.at[start + b]
            if b == b_on:
                hops.append(wires.start(block, block, onward))
        pair = image.at[pl.ds(start, sub)]
        sends.append([wires.start(pair, pair, twin)])
    far = (shifted(x, 2) * 2 + core) * sub
    for b in (0, 1):
        hops[b].wait_recv()
        block = image.at[far + b]
        sends.append([wires.start(block, block, twin)])
    for b in (0, 1):
        sends[b][2].wait_recv()
    for copies in sends[2:]:
        copies[0].wait_recv()
    wires.drain()


def sum_image(part):
    blocks, width, depth = part.shape
    f32 = jnp.float32
    return pl.pallas_call(
        image_kernel,
        out_shape=jax.ShapeDtypeStruct((blocks, depth, width), jnp.bfloat16),
        in_specs=[VMEM],
        out_specs=VMEM,
        scratch_shapes=[
            pltpu.VMEM((RING, 2, width, depth), f32),
            pltpu.VMEM((RING, 2, width, depth), f32),
            pltpu.VMEM((2, width, depth), f32),
            pltpu.VMEM((2, width, depth), f32),
            pltpu.VMEM((2, 2, width, depth), f32),
            pltpu.SemaphoreType.DMA((IMAGE_COPIES,)),
            pltpu.SemaphoreType.DMA((IMAGE_COPIES,)),
        ],
        compiler_params=pltpu.CompilerParams(
            collective_id=1, has_side_effects=True, vmem_limit_bytes=32 << 20
        ),
    )(part)


SCATTER_COPIES = 36


def scatter_sum(plane, wires, part, out, relayed, merged, final, total, hop, joined, close):
    def block(h, first, second):
        return plane.row(h, first, second) * 2 + h

    ups, downs = (2, 1), (3, 0)
    ways = ((0, 1, ups, downs), (1, 3, downs, ups))
    relay, flow = {}, {}
    for h in (0, 1):
        for way, step, onward, plain in ways:
            for slot, s in enumerate(onward):
                relay[h, way, slot] = wires.start(
                    part.at[block(h, 2, s)], relayed.at[h, way, slot], plane.device(h, step, 0)
                )
    for slot in (0, 1):
        for h in (0, 1):
            for way, step, onward, plain in ways:
                s = plain[slot]
                flow[h, way, s] = wires.start(
                    part.at[block(h, step, s)], final.at[h, way, s], plane.device(h, step, 0)
                )
    for slot in (0, 1):
        for h in (0, 1):
            for way, step, onward, plain in ways:
                s = onward[slot]
                relay[h, way, slot].wait_recv()
                merged[h, way, slot] = part[block(h, step, s)] + relayed[h, way, slot]
                flow[h, way, s] = wires.start(
                    merged.at[h, way, slot], final.at[h, way, s], plane.device(h, step, 0)
                )
    cut = out.shape[1] // 2
    low, high = pl.ds(0, cut), pl.ds(cut, cut)
    steps = ((0, 1, low, high), (1, 3, high, low))
    near, direct, ended = {}, {}, {}
    for s in (2, 3, 1, 0):
        for h in (0, 1):
            flow[h, 0, s].wait_recv()
            flow[h, 1, s].wait_recv()
            total[h, s] = part[block(h, 0, s)] + (final[h, 0, s] + final[h, 1, s])
            for way, step, onward, plain in steps:
                if s == 2:
                    near[h, way] = wires.start(
                        total.at[h, 2, onward], hop.at[h, way], plane.device(h, 0, step)
                    )
                elif s == step:
                    direct[h, way] = wires.start(
                        total.at[h, s, plain], close.at[h, way, plain], plane.device(h, 0, step)
                    )
    for h in (0, 1):
        for way, step, onward, plain in steps:
            near[h, way].wait_recv()
            joined[h, way] = total[h, step, onward] + hop[h, way]
            ended[h, way] = wires.start(
                joined.at[h, way], close.at[h, way, onward], plane.device(h, 0, step)
            )
    for h in (0, 1):
        for way in (0, 1):
            direct[h, way].wait_recv()
            ended[h, way].wait_recv()
        out[h] = total[h, 0] + (close[h, 0] + close[h, 1])


def scatter_rooms(depth, width):
    f32 = jnp.float32
    return [
        pltpu.VMEM((2, 2, 2, depth, width), f32),
        pltpu.VMEM((2, 2, 2, depth, width), f32),
        pltpu.VMEM((2, 2, RING, depth, width), f32),
        pltpu.VMEM((2, RING, depth, width), f32),
        pltpu.VMEM((2, 2, depth // 2, width), f32),
        pltpu.VMEM((2, 2, depth // 2, width), f32),
        pltpu.VMEM((2, 2, depth, width), f32),
    ]


SQUARE_COPIES = 7 + 15 + 7


def sum_square(wires, part, out, by_col, by_row, mine):
    rows, cols = lax.axis_size("rows"), lax.axis_size("cols")
    row, col = lax.axis_index("rows"), lax.axis_index("cols")
    share = part.shape[0] // cols

    def span(at):
        return pl.ds(at * share, share)

    first = []
    for o in range(1, cols):
        peer = lax.rem(col + o, cols)
        first.append(wires.start(part.at[span(peer)], by_col.at[col], (row, peer)))
    by_col[col] = part[span(col)]
    for copy in first:
        copy.wait_recv()
    mine[...] = jnp.sum(by_col[...], axis=0)
    second = []
    for o in range(1, rows):
        second.append(wires.start(mine, by_row.at[row], (lax.rem(row + o, rows), col)))
    by_row[row] = mine[...]
    for copy in second:
        copy.wait_recv()
    out[span(col)] = jnp.sum(by_row[...], axis=0)
    third = []
    for o in range(1, cols):
        third.append(
            wires.start(out.at[span(col)], out.at[span(col)], (row, lax.rem(col + o, cols)))
        )
    for copy in third:
        copy.wait_recv()


def square_rooms(order, rows, cols):
    share = order // cols
    return [
        pltpu.VMEM((cols, share, order), jnp.float32),
        pltpu.VMEM((rows, share, order), jnp.float32),
        pltpu.VMEM((share, order), jnp.float32),
    ]


def all_peers():
    rows, cols = lax.axis_size("rows"), lax.axis_size("cols")
    row, col = lax.axis_index("rows"), lax.axis_index("cols")
    return [(lax.rem(row + o, rows), col) for o in range(1, rows)] + [
        (row, lax.rem(col + o, cols)) for o in range(1, cols)
    ]


def fetch_live(count, values, tiles, sems):
    def start(slot, carry):
        pltpu.make_async_copy(values.at[slot], tiles.at[slot], sems.at[slot]).start()
        return carry

    lax.fori_loop(0, count, start, 0)


def forward_kernel(count_ref, row_ref, col_ref, basis, values, out, tiles, sems):
    count = count_ref[0]
    fetch_live(count, values, tiles, sems)
    out[...] = jnp.zeros_like(out)

    def step(slot, carry):
        pltpu.make_async_copy(values.at[slot], tiles.at[slot], sems.at[slot]).wait()
        term = jnp.dot(tiles[slot], basis[col_ref[slot]], preferred_element_type=jnp.float32)
        out[row_ref[slot]] += term
        return carry

    lax.fori_loop(0, count, step, 0)


def backward_kernel(count_ref, row_ref, col_ref, image, values, out, tiles, sems):
    count = count_ref[0]
    fetch_live(count, values, tiles, sems)
    out[...] = jnp.zeros_like(out)

    def step(slot, carry):
        pltpu.make_async_copy(values.at[slot], tiles.at[slot], sems.at[slot]).wait()
        term = jnp.dot(image[row_ref[slot]], tiles[slot], preferred_element_type=jnp.float32)
        out[col_ref[slot]] += term
        return carry

    lax.fori_loop(0, count, step, 0)


def products(kernel, out_shape, count, rows, cols, panels, values):
    return pl.pallas_call(
        kernel,
        out_shape=jax.ShapeDtypeStruct(out_shape, jnp.float32),
        in_specs=[SMEM, SMEM, SMEM, VMEM, ANY],
        out_specs=VMEM,
        scratch_shapes=[
            pltpu.VMEM(values.shape, values.dtype),
            pltpu.SemaphoreType.DMA((values.shape[0],)),
        ],
        compiler_params=pltpu.CompilerParams(vmem_limit_bytes=32 << 20),
    )(count, rows, cols, panels, values)


def factor(gram, upper_ref, inverse_ref):
    order = gram.shape[0]
    lead = gram
    tail = (
        lax.broadcasted_iota(jnp.int32, (order, order), 0)
        == lax.broadcasted_iota(jnp.int32, (order, order), 1)
    ).astype(jnp.float32)
    for base in range(0, order, SUB):
        left = order - base
        columns = [
            jnp.broadcast_to(lead[:, base + k : base + k + 1], (left, order)) for k in range(SUB)
        ]
        position = lax.broadcasted_iota(jnp.int32, (left, order), 0)
        top = lax.broadcasted_iota(jnp.int32, (SUB, order), 0)
        lane = lax.broadcasted_iota(jnp.int32, (SUB, order), 1)
        pivots = jnp.zeros((SUB, order), jnp.float32)
        for k in range(SUB):
            pivot = columns[k][k : k + 1, :]
            pivots = jnp.where(top == k, pivot, pivots)
            ratio = jnp.where(position > k, columns[k] * (1.0 / pivot), 0.0)
            lead = lead - ratio * lead[k : k + 1, :]
            tail = tail - ratio * tail[k : k + 1, :]
            for j in range(k + 1, SUB):
                columns[j] = columns[j] - ratio * columns[j][k : k + 1, :]
        scale = 1.0 / jnp.sqrt(pivots)
        upper_ref[base : base + SUB, :] = jnp.where(lane >= base + top, lead[:SUB] * scale, 0.0)
        inverse_ref[base : base + SUB, :] = tail[:SUB] * scale
        lead = lead[SUB:]
        tail = tail[SUB:]


def inner(x_ref, out):
    out[...] = matmul(x_ref[0], x_ref[0], NT) + matmul(x_ref[1], x_ref[1], NT)


def basis_kernel(
    root, part, basis_ref, triangle_ref, x_ref, square, gram, upper, second, inverse, *rest
):
    rooms, (by_col, by_row, mine, by_col2, by_row2, mine2, send, recv) = rest[:7], rest[7:]
    plane = Plane()
    wires = Wires(send, recv)
    greet(all_peers())
    scatter_sum(plane, wires, part, x_ref, *rooms)
    inner(x_ref, square)
    sum_square(wires, square, gram, by_col, by_row, mine)
    factor(gram[...], upper, inverse)
    for s in range(2):
        x_ref[s] = matmul(inverse[...], x_ref[s], NN)
    wires.drain()
    wires = Wires(send, recv)
    wires.send = send.at[pl.ds(SCATTER_COPIES + SQUARE_COPIES, SQUARE_COPIES)]
    wires.recv = recv.at[pl.ds(SCATTER_COPIES + SQUARE_COPIES, SQUARE_COPIES)]
    inner(x_ref, square)
    sum_square(wires, square, gram, by_col2, by_row2, mine2)
    factor(gram[...], second, inverse)
    width = x_ref.shape[2]
    for s in range(2):
        basis_ref[s * width : (s + 1) * width, :] = matmul(inverse[...], x_ref[s], NN).T * root
    triangle_ref[...] = matmul(second[...], upper[...], NN) / root
    wires.drain()


def orthonormalize(root, part):
    _, depth, width = part.shape
    rows, cols = lax.axis_size("rows"), lax.axis_size("cols")
    copies = SCATTER_COPIES + 2 * SQUARE_COPIES
    f32 = jnp.float32
    square = pltpu.VMEM((depth, depth), f32)
    return pl.pallas_call(
        functools.partial(basis_kernel, root),
        out_shape=[
            jax.ShapeDtypeStruct((2 * width, depth), f32),
            jax.ShapeDtypeStruct((depth, depth), f32),
        ],
        in_specs=[VMEM],
        out_specs=[VMEM] * 2,
        scratch_shapes=[pltpu.VMEM((2, depth, width), f32)]
        + [square] * 5
        + scatter_rooms(depth, width)
        + square_rooms(depth, rows, cols) * 2
        + [pltpu.SemaphoreType.DMA((copies,)), pltpu.SemaphoreType.DMA((copies,))],
        compiler_params=pltpu.CompilerParams(
            collective_id=2, has_side_effects=True, vmem_limit_bytes=40 << 20
        ),
    )(part)


def body(start_basis, block_values, slot_count, slot_row, slot_col):
    depth = start_basis.shape[1]
    width = block_values.shape[-1]
    panel_blocks = start_basis.shape[0] // width
    rows, cols = lax.axis_size("rows"), lax.axis_size("cols")
    sub_blocks = panel_blocks // cols
    own = lax.dynamic_slice_in_dim(
        start_basis.reshape(panel_blocks, width, depth),
        lax.axis_index("cols") * sub_blocks,
        sub_blocks,
        0,
    )
    basis_parts = gather(own, rows).reshape(rows * sub_blocks, width, depth)
    values = block_values[0, 0]
    count = slot_count[0]
    row_ids = slot_row[0, 0]
    col_ids = slot_col[0, 0]
    local_cols = col_ids // panel_blocks * sub_blocks + col_ids % sub_blocks
    image_part = products(
        forward_kernel, (panel_blocks, width, depth), count, row_ids, local_cols, basis_parts, values
    )
    image = sum_image(image_part)
    back_part = products(
        backward_kernel, (rows * sub_blocks, depth, width), count, row_ids, local_cols, image, values
    )
    return tuple(orthonormalize(float(rows * panel_blocks * width) ** 0.5, back_part))


def solution(mesh):
    return jax.shard_map(
        body,
        mesh=mesh,
        in_specs=(
            P("rows", None),
            P("rows", "cols", None, None, None),
            P("rows", "cols"),
            P("rows", "cols", None),
            P("rows", "cols", None),
        ),
        out_specs=(P(("rows", "cols"), None), P()),
        check_vma=False,
    )
```

time: 513 us -> 138 us (0.27)
  waiting for transfers between devices: 407 us -> 0 us
  Pallas kernels: 28.2 us -> 131 us
  blocking collectives: 51.1 us -> 0 us
  between operations: 14.5 us -> 1.45 us
  local copies, waits for them, and re-layouts: 11.6 us -> 4.69 us
    psum x2 -> x0, waiting for transfers between devices: 277 us -> none  [body(): gram = lax.psum(part, ('rows', 'cols'))]
    pallas_call x5, Pallas kernels: 28.2 us -> 131 us  [the longest x1 73.4 us: orthonormalize(): pl.pallas_call(functools.partial(basis_kernel, root), out_shape=[jax.Shap...]
    reduce_scatter x1 -> x0, waiting for transfers between devices: 81.5 us -> none  [body(): mine = lax.psum_scatter(back_part, 'rows', scatter_dimension=0, tiled=True)]
    psum x1 -> x0, blocking collectives: 51.1 us -> none  [body(): image = lax.psum(image_part, 'cols').astype(jnp.bfloat16)]
    all_gather x1 -> x0, waiting for transfers between devices: 47.8 us -> none  [body(): lax.all_gather(own_part, 'rows', axis=0, tiled=True)]
    unnamed x16 -> x12, local copies, waits for them, and re-layouts: 11 us -> 4.68 us
  transfers between devices with their start and end apart: 4 -> 0, of which waited for: 4 -> 0; matrix products, arithmetic and copies ran while one was open for 0% -> 0% of each run, Pallas kernels for 0% -> 0%
where the time goes in v2:
time: 138 us
  Pallas kernels  131 us (95%)
  local copies, waits for them, and re-layouts  4.69 us (3%)
  between operations  1.45 us (1%)
    pallas_call x1, Pallas kernels, orthonormalize(): pl.pallas_call(functools.partial(basis_kernel, root), out_shape=[jax.Shap...  73.4 us
    pallas_call x1, Pallas kernels, sum_image(): pl.pallas_call(image_kernel, out_shape=jax.ShapeDtypeStruct((blocks, dept...  27 us
    pallas_call x1, Pallas kernels, gather(): pl.pallas_call(gather_kernel, out_shape=jax.ShapeDtypeStruct((rows,) + ow...  19.4 us
    pallas_call x2, Pallas kernels, products(): pl.pallas_call(kernel, out_shape=jax.ShapeDtypeStruct(out_shape, jnp.floa...  11.1 us
    unnamed x12, local copies, waits for them, and re-layouts  4.68 us

profile of v2, /device:TPU:1, one launch (start us, length us, event | category | flops | bytes accessed | tf_op | source)
XLA Modules:
  0.0 137.7 jit_solution(15455865749067814091)
XLA Ops:
  0.6 0.0 copy-start
  1.4 0.5 copy-done
  1.9 0.7 fusion.col_ref
  2.6 19.4 %shard_map.68 = bf16[16,2,256,128]{3,2,1,0:T(8,128)(2,1)S(1)} custom-call(bf16[2,256,128]{2,1,0:T(8,128)(2,1)S(1)} %constant_dynamic-slice_fusion.own), custom_call_target="tpu_custom_call" | custom-call | tf_op jit(solution)/shard_map/pallas_call | solution.py:134
  21.9 0.0 copy-start.1
  22.0 2.2 %copy-done.1 = bf16[1,1,32,256,256]{4,3,2,1,0:T(8,128)(2,1)S(1)} copy-done((bf16[1,1,32,256,256]{4,3,2,1,0:T(8,128)(2,1)S(1)}, bf16[1,1,32,256,256]{4,3,2,1,0:T(8,128)(2,1)}, u32[]{:S(2)}) %copy-start.1) | copy-done | bytes 4194328
  24.1 0.0 copy-start.3
  24.1 0.7 copy-done.3
  24.8 0.0 copy-start.2
  24.8 0.0 copy-start.4
  24.8 5.6 %shard_map.69.part = f32[16,256,128]{2,1,0:T(8,128)S(1)} custom-call(s32[1]{0:T(128)} %bitcast.16.count_ref, s32[32]{0:T(128)S(1)} %bitcast.22, s32[32]{0:T(128)S(1)} %fusion.col_ref, bf16[32,256,128]{2,1,0:T(8,128)(2,1)S(1)} %bitcast.21, bf16[32,256,256]{2,1,0:T(8,128)(2,1)S(1)} %bitcast.19), custom_call_target="tpu_custom_call" | custom-call | tf_op jit(solution)/shard_map/pallas_call | solution.py:409
  30.4 27.0 %shard_map.70.image = bf16[16,128,256]{2,1,0:T(8,128)(2,1)S(1)} custom-call(f32[16,256,128]{2,1,0:T(8,128)S(1)} %shard_map.69.part), custom_call_target="tpu_custom_call" | custom-call | tf_op jit(solution)/shard_map/pallas_call | solution.py:223
  57.4 0.0 copy-done.2
  57.4 0.0 copy-done.4
  57.4 5.6 %shard_map.71.part = f32[32,128,256]{2,1,0:T(8,128)S(1)} custom-call(s32[1]{0:T(128)} %bitcast.17.count_ref, s32[32]{0:T(128)S(1)} %bitcast.23, s32[32]{0:T(128)S(1)} %fusion.col_ref, bf16[16,128,256]{2,1,0:T(8,128)(2,1)S(1)} %shard_map.70.image, bf16[32,256,256]{2,1,0:T(8,128)(2,1)S(1)} %bitcast.20), custom_call_target="tpu_custom_call" | custom-call | tf_op jit(solution)/shard_map/pallas_call | solution.py:409
  63.0 73.4 %shard_map.72 = (f32[512,128]{1,0:T(8,128)S(1)}, f32[128,128]{1,0:T(8,128)S(1)}) custom-call(f32[32,128,256]{2,1,0:T(8,128)S(1)} %shard_map.71.part), custom_call_target="tpu_custom_call" | custom-call | tf_op jit(solution)/shard_map/pallas_call | solution.py:490
  136.4 0.7 copy.10
  137.1 0.6 copy.11
  (1 shorter events, 0.0 us)
Async XLA Ops:
  0.6 1.2 copy-start
  21.9 2.2 %copy-start.1 = (bf16[1,1,32,256,256]{4,3,2,1,0:T(8,128)(2,1)S(1)}, bf16[1,1,32,256,256]{4,3,2,1,0:T(8,128)(2,1)}, u32[]{:S(2)}) copy-start(bf16[1,1,32,256,256]{4,3,2,1,0:T(8,128)(2,1)} %param.6) | copy-start | bytes 12582916
  24.1 0.7 copy-start.3
  24.8 32.6 %copy-start.2 = (bf16[1,1,32,256,256]{4,3,2,1,0:T(8,128)(2,1)S(1)}, bf16[1,1,32,256,256]{4,3,2,1,0:T(8,128)(2,1)}, u32[]{:S(2)}) copy-start(bf16[1,1,32,256,256]{4,3,2,1,0:T(8,128)(2,1)} %param.6) | copy-start | bytes 12582916
  24.8 32.6 %copy-start.4 = (s32[1,1,32]{2,1,0:T(1,128)S(1)}, s32[1,1,32]{2,1,0:T(1,128)}, u32[]{:S(2)}) copy-start(s32[1,1,32]{2,1,0:T(1,128)} %param.8) | copy-start | bytes 388

commit v3 on v2

--- a/solution.py
+++ b/solution.py
@@ -11,7 +11,7 @@
 RING = 4
 VMEM = pl.BlockSpec(memory_space=pltpu.VMEM)
 SMEM = pl.BlockSpec(memory_space=pltpu.SMEM)
-ANY = pl.BlockSpec(memory_space=pl.ANY)
+HBM = pl.BlockSpec(memory_space=pltpu.HBM)
 NN = (((1,), (0,)), ((), ()))
 NT = (((1,), (1,)), ((), ()))
 
@@ -24,25 +24,26 @@
 
 class Wires:
     def __init__(self, send, recv):
-        self.send, self.recv, self.used = send, recv, []
-
-    def start(self, src, dst, device):
-        at = len(self.used)
+        self.send, self.recv, self.used = send, recv, 0
+
+    def start(self, src, dst, device, at=None):
+        if at is None:
+            at = self.used
+            self.used += 1
         copy = pltpu.make_async_remote_copy(
             src_ref=src,
             dst_ref=dst,
-            send_sem=self.send.at[at],
+            send_sem=self.send,
             recv_sem=self.recv.at[at],
             device_id=device,
             device_id_type=pl.DeviceIdType.MESH,
         )
         copy.start()
-        self.used.append(copy)
         return copy
 
-    def drain(self):
-        for copy in self.used:
-            copy.wait_send()
+    def drain(self, *refs):
+        for ref in refs:
+            pltpu.make_async_copy(ref, ref, self.send).wait()
 
 
 def greet(peers):
@@ -75,82 +76,95 @@
         return [self.device(0, 1, 0), self.device(0, 3, 0), self.device(0, 0, 1), self.device(0, 0, 3)]
 
 
-GATHER_COPIES = 40
-
-
-def gather_kernel(own, out, send, recv, local):
+GATHER_COPIES = 24
+
+
+def gather_kernel(basis, values, out, tiles, send, recv, local):
     plane = Plane()
     wires = Wires(send, recv)
-    me = plane.row(0, 0, 0)
-    keep = pltpu.make_async_copy(own, out.at[me], local)
+    load = pltpu.make_async_copy(basis.at[pl.ds(plane.col * 2, 2)], out.at[:, 0, 0], local.at[0])
+    load.start()
+    keep = pltpu.make_async_copy(values, tiles, local.at[1])
     keep.start()
     greet(plane.neighbours())
-    cut = own.shape[1] // 2
+    load.wait()
+    cut = out.shape[3] // 2
     upper, lower = pl.ds(0, cut), pl.ds(cut, cut)
-
-    def both_ways(half, first, axis, src):
-        dst = out.at[plane.row(half, first, 0), half]
-        if axis == 0:
-            return [wires.start(src, dst, plane.device(half, s, 0)) for s in (1, 3)]
-        return [wires.start(src, dst, plane.device(half, 0, s)) for s in (1, 3)]
-
-    along_first = [both_ways(h, 0, 0, own.at[h]) for h in (0, 1)]
-    along_second = {(h, 0): both_ways(h, 0, 1, own.at[h]) for h in (0, 1)}
-    relays = []
-    for h in (0, 1):
-        pair = []
-        for at, (come_from, part, onward) in enumerate(((3, upper, 1), (1, lower, 3))):
-            along_first[h][at].wait_recv()
-            piece = out.at[plane.row(h, come_from, 0), h, part]
-            pair.append(wires.start(piece, piece, plane.device(h, onward, 0)))
-        relays.append(pair)
-    for h in (0, 1):
-        for f in (3, 1):
-            along_second[h, f] = both_ways(h, f, 1, out.at[plane.row(h, f, 0), h])
-    last = []
-
-    def pass_on(h, f):
-        for at, (come_from, part, onward) in enumerate(((3, upper, 1), (1, lower, 3))):
-            along_second[h, f][at].wait_recv()
-            piece = out.at[plane.row(h, f, come_from), h, part]
-            last.append(wires.start(piece, piece, plane.device(h, 0, onward)))
-
-    for h in (0, 1):
-        pass_on(h, 0)
-    for h in (0, 1):
-        for copy in relays[h]:
+    near, own, rest, relay, far, ends = {}, {}, {}, {}, {}, {}
+    for h in (0, 1):
+        src = out.at[h, 0, 0]
+        near[h] = [
+            wires.start(src, out.at[h, 3, 0], plane.device(h, 1, 0)),
+            wires.start(src, out.at[h, 1, 0], plane.device(h, 3, 0)),
+        ]
+    for h in (0, 1):
+        src = out.at[h, 0, 0]
+        own[h] = [
+            wires.start(src, out.at[h, 0, 3], plane.device(h, 0, 1)),
+            wires.start(src, out.at[h, 0, 1], plane.device(h, 0, 3)),
+        ]
+    for h in (0, 1):
+        near[h][0].wait_recv()
+        up = wires.start(out.at[h, 3, 0, upper], out.at[h, 2, 0, upper], plane.device(h, 1, 0))
+        near[h][1].wait_recv()
+        down = wires.start(out.at[h, 1, 0, lower], out.at[h, 2, 0, lower], plane.device(h, 3, 0))
+        relay[h] = [up, down]
+    for h in (0, 1):
+        own[h][0].wait_recv()
+        up = wires.start(out.at[h, 0, 3, upper], out.at[h, 0, 2, upper], plane.device(h, 0, 1))
+        own[h][1].wait_recv()
+        down = wires.start(out.at[h, 0, 1, lower], out.at[h, 0, 2, lower], plane.device(h, 0, 3))
+        far[h] = [up, down]
+    three = pl.ds(1, 3)
+    for h in (0, 1):
+        relay[h][0].wait_recv()
+        relay[h][1].wait_recv()
+        src = out.at[h, three, 0]
+        rest[h] = [
+            wires.start(src, out.at[h, three, 3], plane.device(h, 0, 1)),
+            wires.start(src, out.at[h, three, 1], plane.device(h, 0, 3)),
+        ]
+    for h in (0, 1):
+        rest[h][0].wait_recv()
+        up = wires.start(
+            out.at[h, three, 3, upper], out.at[h, three, 2, upper], plane.device(h, 0, 1)
+        )
+        rest[h][1].wait_recv()
+        down = wires.start(
+            out.at[h, three, 1, lower], out.at[h, three, 2, lower], plane.device(h, 0, 3)
+        )
+        ends[h] = [up, down]
+    for h in (0, 1):
+        for copy in far[h] + ends[h]:
             copy.wait_recv()
-        along_second[h, 2] = both_ways(h, 2, 1, out.at[plane.row(h, 2, 0), h])
-    for f in (3, 1, 2):
-        for h in (0, 1):
-            pass_on(h, f)
-    for copy in last:
-        copy.wait_recv()
     keep.wait()
-    wires.drain()
-
-
-def gather(own, rows):
+    wires.drain(out.at[0], out.at[1, pl.ds(0, 3)], out.at[1, 3, pl.ds(0, 2)])
+
+
+def gather(basis, values, rows):
     return pl.pallas_call(
         gather_kernel,
-        out_shape=jax.ShapeDtypeStruct((rows,) + own.shape, own.dtype),
-        in_specs=[VMEM],
-        out_specs=VMEM,
+        out_shape=[
+            jax.ShapeDtypeStruct((2, rows // RING, RING) + basis.shape[1:], basis.dtype),
+            jax.ShapeDtypeStruct(values.shape, values.dtype),
+        ],
+        in_specs=[HBM, HBM],
+        out_specs=[VMEM, VMEM],
         scratch_shapes=[
+            pltpu.SemaphoreType.DMA,
             pltpu.SemaphoreType.DMA((GATHER_COPIES,)),
-            pltpu.SemaphoreType.DMA((GATHER_COPIES,)),
-            pltpu.SemaphoreType.DMA,
+            pltpu.SemaphoreType.DMA((2,)),
         ],
         compiler_params=pltpu.CompilerParams(
-            collective_id=0, has_side_effects=True, vmem_limit_bytes=32 << 20
+            collective_id=0, has_side_effects=True, vmem_limit_bytes=44 << 20
         ),
-    )(own)
+    )(basis, values)
 
 
 IMAGE_COPIES = 24
 
 
-def image_kernel(part, image, sibling, total, relayed, merged, final, send, recv):
+def image_kernel(part, image, sibling, total, relayed, merged, final, send, recv, send2):
     row, col = lax.axis_index("rows"), lax.axis_index("cols")
     x, core = col // 2, lax.rem(col, 2)
     twin = (row, x * 2 + 1 - core)
@@ -183,6 +197,7 @@
     merged[1] = total[3, 1] + relayed[1]
     left_sum = wires.start(merged.at[1], final.at[1, 1], left)
 
+    wires.send = send2
     mine = (x * 2 + core) * sub
     left_plain.wait_recv()
     right_sum.wait_recv()
@@ -214,7 +229,9 @@
         sends[b][2].wait_recv()
     for copies in sends[2:]:
         copies[0].wait_recv()
-    wires.drain()
+    wires.drain(image.at[pl.ds(0, 14)])
+    wires.send = send
+    wires.drain(part.at[pl.ds(0, 14)])
 
 
 def sum_image(part):
@@ -231,8 +248,9 @@
             pltpu.VMEM((2, width, depth), f32),
             pltpu.VMEM((2, width, depth), f32),
             pltpu.VMEM((2, 2, width, depth), f32),
+            pltpu.SemaphoreType.DMA,
             pltpu.SemaphoreType.DMA((IMAGE_COPIES,)),
-            pltpu.SemaphoreType.DMA((IMAGE_COPIES,)),
+            pltpu.SemaphoreType.DMA,
         ],
         compiler_params=pltpu.CompilerParams(
             collective_id=1, has_side_effects=True, vmem_limit_bytes=32 << 20
@@ -245,7 +263,7 @@
 
 def scatter_sum(plane, wires, part, out, relayed, merged, final, total, hop, joined, close):
     def block(h, first, second):
-        return plane.row(h, first, second) * 2 + h
+        return (h * RING + first) * RING + second
 
     ups, downs = (2, 1), (3, 0)
     ways = ((0, 1, ups, downs), (1, 3, downs, ups))
@@ -317,39 +335,43 @@
     ]
 
 
-SQUARE_COPIES = 7 + 15 + 7
+SQUARE_STEPS = 3
 
 
 def sum_square(wires, part, out, by_col, by_row, mine):
     rows, cols = lax.axis_size("rows"), lax.axis_size("cols")
     row, col = lax.axis_index("rows"), lax.axis_index("cols")
     share = part.shape[0] // cols
+    at = wires.used
+    wires.used += SQUARE_STEPS
 
     def span(at):
         return pl.ds(at * share, share)
 
-    first = []
+    def arrived(ref, step):
+        pltpu.make_async_copy(ref, ref, wires.recv.at[at + step]).wait()
+
     for o in range(1, cols):
         peer = lax.rem(col + o, cols)
-        first.append(wires.start(part.at[span(peer)], by_col.at[col], (row, peer)))
+        wires.start(part.at[span(peer)], by_col.at[col], (row, peer), at)
     by_col[col] = part[span(col)]
-    for copy in first:
-        copy.wait_recv()
+    arrived(by_col.at[pl.ds(0, cols - 1)], 0)
     mine[...] = jnp.sum(by_col[...], axis=0)
-    second = []
     for o in range(1, rows):
-        second.append(wires.start(mine, by_row.at[row], (lax.rem(row + o, rows), col)))
+        wires.start(mine, by_row.at[row], (lax.rem(row + o, rows), col), at + 1)
     by_row[row] = mine[...]
-    for copy in second:
-        copy.wait_recv()
+    arrived(by_row.at[pl.ds(0, rows - 1)], 1)
     out[span(col)] = jnp.sum(by_row[...], axis=0)
-    third = []
     for o in range(1, cols):
-        third.append(
-            wires.start(out.at[span(col)], out.at[span(col)], (row, lax.rem(col + o, cols)))
+        wires.start(
+            out.at[span(col)], out.at[span(col)], (row, lax.rem(col + o, cols)), at + 2
         )
-    for copy in third:
-        copy.wait_recv()
+    arrived(out.at[pl.ds(0, (cols - 1) * share)], 2)
+    wires.drain(
+        by_col.at[pl.ds(0, cols - 1)],
+        by_row.at[pl.ds(0, rows - 1)],
+        out.at[pl.ds(0, (cols - 1) * share)],
+    )
 
 
 def square_rooms(order, rows, cols):
@@ -369,54 +391,52 @@
     ]
 
 
-def fetch_live(count, values, tiles, sems):
-    def start(slot, carry):
-        pltpu.make_async_copy(values.at[slot], tiles.at[slot], sems.at[slot]).start()
+GROUP = 8
+
+
+def local_column(column):
+    row = lax.axis_index("rows")
+    panel, half = column // 16, lax.rem(column, 2)
+    along_z = lax.rem(panel // RING + RING - row // RING, RING)
+    along_y = lax.rem(lax.rem(panel, RING) + RING - lax.rem(row, RING), RING)
+    first = jnp.where(half == 0, along_y, along_z)
+    second = jnp.where(half == 0, along_z, along_y)
+    return (half * RING + first) * RING + second
+
+
+def products_kernel(transposed, count_ref, row_ref, col_ref, panels, tiles, out):
+    count = count_ref[0, 0]
+    out[...] = jnp.zeros_like(out)
+
+    def step(group, carry):
+        slots = [group * GROUP + u for u in range(GROUP)]
+        rows = [row_ref[0, 0, slot] for slot in slots]
+        cols = [local_column(col_ref[0, 0, slot]) for slot in slots]
+        if transposed:
+            terms = [
+                jnp.dot(panels[r], tiles[slot], preferred_element_type=jnp.float32)
+                for r, slot in zip(rows, slots)
+            ]
+        else:
+            terms = [
+                jnp.dot(tiles[slot], panels[c], preferred_element_type=jnp.float32)
+                for c, slot in zip(cols, slots)
+            ]
+        for slot, term, place in zip(slots, terms, cols if transposed else rows):
+            out[place] += jnp.where(slot < count, term, 0.0)
         return carry
 
-    lax.fori_loop(0, count, start, 0)
-
-
-def forward_kernel(count_ref, row_ref, col_ref, basis, values, out, tiles, sems):
-    count = count_ref[0]
-    fetch_live(count, values, tiles, sems)
-    out[...] = jnp.zeros_like(out)
-
-    def step(slot, carry):
-        pltpu.make_async_copy(values.at[slot], tiles.at[slot], sems.at[slot]).wait()
-        term = jnp.dot(tiles[slot], basis[col_ref[slot]], preferred_element_type=jnp.float32)
-        out[row_ref[slot]] += term
-        return carry
-
-    lax.fori_loop(0, count, step, 0)
-
-
-def backward_kernel(count_ref, row_ref, col_ref, image, values, out, tiles, sems):
-    count = count_ref[0]
-    fetch_live(count, values, tiles, sems)
-    out[...] = jnp.zeros_like(out)
-
-    def step(slot, carry):
-        pltpu.make_async_copy(values.at[slot], tiles.at[slot], sems.at[slot]).wait()
-        term = jnp.dot(image[row_ref[slot]], tiles[slot], preferred_element_type=jnp.float32)
-        out[col_ref[slot]] += term
-        return carry
-
-    lax.fori_loop(0, count, step, 0)
-
-
-def products(kernel, out_shape, count, rows, cols, panels, values):
+    lax.fori_loop(0, (count + GROUP - 1) // GROUP, step, 0)
+
+
+def products(transposed, out_shape, count, rows, cols, panels, tiles):
     return pl.pallas_call(
-        kernel,
+        functools.partial(products_kernel, transposed),
         out_shape=jax.ShapeDtypeStruct(out_shape, jnp.float32),
-        in_specs=[SMEM, SMEM, SMEM, VMEM, ANY],
+        in_specs=[SMEM, SMEM, SMEM, VMEM, VMEM],
         out_specs=VMEM,
-        scratch_shapes=[
-            pltpu.VMEM(values.shape, values.dtype),
-            pltpu.SemaphoreType.DMA((values.shape[0],)),
-        ],
         compiler_params=pltpu.CompilerParams(vmem_limit_bytes=32 << 20),
-    )(count, rows, cols, panels, values)
+    )(count, rows, cols, panels, tiles)
 
 
 def factor(gram, upper_ref, inverse_ref):
@@ -455,36 +475,36 @@
 
 
 def basis_kernel(
-    root, part, basis_ref, triangle_ref, x_ref, square, gram, upper, second, inverse, *rest
+    root, part, basis_ref, triangle_ref, spread_ref, x_ref, square, gram, inverse, *rest
 ):
-    rooms, (by_col, by_row, mine, by_col2, by_row2, mine2, send, recv) = rest[:7], rest[7:]
+    rooms, (by_col, by_row, mine, send, recv, send2) = rest[:7], rest[7:]
     plane = Plane()
     wires = Wires(send, recv)
     greet(all_peers())
     scatter_sum(plane, wires, part, x_ref, *rooms)
     inner(x_ref, square)
+    wires.send = send2
     sum_square(wires, square, gram, by_col, by_row, mine)
-    factor(gram[...], upper, inverse)
-    for s in range(2):
-        x_ref[s] = matmul(inverse[...], x_ref[s], NN)
-    wires.drain()
-    wires = Wires(send, recv)
-    wires.send = send.at[pl.ds(SCATTER_COPIES + SQUARE_COPIES, SQUARE_COPIES)]
-    wires.recv = recv.at[pl.ds(SCATTER_COPIES + SQUARE_COPIES, SQUARE_COPIES)]
-    inner(x_ref, square)
-    sum_square(wires, square, gram, by_col2, by_row2, mine2)
-    factor(gram[...], second, inverse)
+    factor(gram[...], triangle_ref, inverse)
     width = x_ref.shape[2]
     for s in range(2):
         basis_ref[s * width : (s + 1) * width, :] = matmul(inverse[...], x_ref[s], NN).T * root
-    triangle_ref[...] = matmul(second[...], upper[...], NN) / root
-    wires.drain()
+    triangle_ref[...] = triangle_ref[...] / root
+    order = gram.shape[0]
+    diagonal = lax.broadcasted_iota(jnp.int32, (order, order), 0) == lax.broadcasted_iota(
+        jnp.int32, (order, order), 1
+    )
+    lengths = jnp.sum(jnp.where(diagonal, gram[...], 0.0), axis=0, keepdims=True)
+    inverses = jnp.sum(inverse[...] * inverse[...], axis=0, keepdims=True)
+    spread = jnp.sum(lengths * inverses, axis=1, keepdims=True)
+    spread_ref[...] = jnp.broadcast_to(spread, spread_ref.shape)
+    wires.send = send
+    wires.drain(part.at[pl.ds(0, 30)])
 
 
 def orthonormalize(root, part):
     _, depth, width = part.shape
     rows, cols = lax.axis_size("rows"), lax.axis_size("cols")
-    copies = SCATTER_COPIES + 2 * SQUARE_COPIES
     f32 = jnp.float32
     square = pltpu.VMEM((depth, depth), f32)
     return pl.pallas_call(
@@ -492,18 +512,58 @@
         out_shape=[
             jax.ShapeDtypeStruct((2 * width, depth), f32),
             jax.ShapeDtypeStruct((depth, depth), f32),
+            jax.ShapeDtypeStruct((SUB, depth), f32),
         ],
         in_specs=[VMEM],
-        out_specs=[VMEM] * 2,
+        out_specs=[VMEM] * 3,
         scratch_shapes=[pltpu.VMEM((2, depth, width), f32)]
-        + [square] * 5
+        + [square] * 3
         + scatter_rooms(depth, width)
-        + square_rooms(depth, rows, cols) * 2
-        + [pltpu.SemaphoreType.DMA((copies,)), pltpu.SemaphoreType.DMA((copies,))],
+        + square_rooms(depth, rows, cols)
+        + [
+            pltpu.SemaphoreType.DMA,
+            pltpu.SemaphoreType.DMA((SCATTER_COPIES + SQUARE_STEPS,)),
+            pltpu.SemaphoreType.DMA,
+        ],
         compiler_params=pltpu.CompilerParams(
             collective_id=2, has_side_effects=True, vmem_limit_bytes=40 << 20
         ),
     )(part)
+
+
+def again_kernel(
+    root, basis_in, triangle_in, basis_ref, triangle_ref, x, square, gram, upper, inverse, *rest
+):
+    by_col, by_row, mine, send, recv = rest
+    wires = Wires(send, recv)
+    greet(all_peers())
+    x[...] = basis_in[...].T / root
+    square[...] = matmul(x[...], x[...], NT)
+    sum_square(wires, square, gram, by_col, by_row, mine)
+    factor(gram[...], upper, inverse)
+    basis_ref[...] = matmul(inverse[...], x[...], NN).T * root
+    triangle_ref[...] = matmul(upper[...], triangle_in[...], NN)
+
+
+def second_pass(root, basis, triangle):
+    size, depth = basis.shape
+    f32 = jnp.float32
+    return pl.pallas_call(
+        functools.partial(again_kernel, root),
+        out_shape=[
+            jax.ShapeDtypeStruct(basis.shape, f32),
+            jax.ShapeDtypeStruct(triangle.shape, f32),
+        ],
+        in_specs=[VMEM] * 2,
+        out_specs=[VMEM] * 2,
+        scratch_shapes=[pltpu.VMEM((depth, size), f32)]
+        + [pltpu.VMEM((depth, depth), f32)] * 4
+        + square_rooms(depth, lax.axis_size("rows"), lax.axis_size("cols"))
+        + [pltpu.SemaphoreType.DMA, pltpu.SemaphoreType.DMA((SQUARE_STEPS,))],
+        compiler_params=pltpu.CompilerParams(
+            collective_id=3, has_side_effects=True, vmem_limit_bytes=32 << 20
+        ),
+    )(basis, triangle)
 
 
 def body(start_basis, block_values, slot_count, slot_row, slot_col):
@@ -511,27 +571,34 @@
     width = block_values.shape[-1]
     panel_blocks = start_basis.shape[0] // width
     rows, cols = lax.axis_size("rows"), lax.axis_size("cols")
-    sub_blocks = panel_blocks // cols
-    own = lax.dynamic_slice_in_dim(
+    column_blocks = rows * panel_blocks // cols
+    basis_parts, tiles = gather(
         start_basis.reshape(panel_blocks, width, depth),
-        lax.axis_index("cols") * sub_blocks,
-        sub_blocks,
-        0,
-    )
-    basis_parts = gather(own, rows).reshape(rows * sub_blocks, width, depth)
-    values = block_values[0, 0]
-    count = slot_count[0]
-    row_ids = slot_row[0, 0]
-    col_ids = slot_col[0, 0]
-    local_cols = col_ids // panel_blocks * sub_blocks + col_ids % sub_blocks
+        block_values.reshape(block_values.shape[2:]),
+        rows,
+    )
     image_part = products(
-        forward_kernel, (panel_blocks, width, depth), count, row_ids, local_cols, basis_parts, values
+        False,
+        (panel_blocks, width, depth),
+        slot_count,
+        slot_row,
+        slot_col,
+        basis_parts.reshape(column_blocks, width, depth),
+        tiles,
     )
     image = sum_image(image_part)
     back_part = products(
-        backward_kernel, (rows * sub_blocks, depth, width), count, row_ids, local_cols, image, values
-    )
-    return tuple(orthonormalize(float(rows * panel_blocks * width) ** 0.5, back_part))
+        True, (column_blocks, depth, width), slot_count, slot_row, slot_col, image, tiles
+    )
+    root = float(rows * panel_blocks * width) ** 0.5
+    basis, triangle, spread = orthonormalize(root, back_part)
+    return lax.cond(
+        spread[0, 0] <= 2.0 * depth,
+        lambda basis, triangle: (basis, triangle),
+        functools.partial(second_pass, root),
+        basis,
+        triangle,
+    )
 
 
 def solution(mesh):

time: 138 us -> 102 us (0.74)
  Pallas kernels: 131 us -> 96.5 us
  local copies, waits for them, and re-layouts: 4.69 us -> 3.07 us
    pallas_call x1, Pallas kernels: 73.4 us -> 45.8 us  [orthonormalize(): pl.pallas_call(functools.partial(basis_kernel, root), out_shape=[jax.Shap...]
    pallas_call x3, Pallas kernels: 30.5 us -> 22.8 us  [the longest x1 20.5 us: gather(): pl.pallas_call(gather_kernel, out_shape=[jax.ShapeDtypeStruct((2, rows //...]
    unnamed x12 -> x8, local copies, waits for them, and re-layouts: 4.68 us -> 2.56 us
where the time goes in v3:
time: 102 us
  Pallas kernels  96.5 us (95%)
  local copies, waits for them, and re-layouts  3.07 us (3%)
  between operations  2.03 us (2%)
    pallas_call x1, Pallas kernels, orthonormalize(): pl.pallas_call(functools.partial(basis_kernel, root), out_shape=[jax.Shap...  45.8 us
    pallas_call x1, Pallas kernels, sum_image(): pl.pallas_call(image_kernel, out_shape=jax.ShapeDtypeStruct((blocks, dept...  27.9 us
    pallas_call x1, Pallas kernels, gather(): pl.pallas_call(gather_kernel, out_shape=[jax.ShapeDtypeStruct((2, rows //...  20.5 us
    unnamed x8, local copies, waits for them, and re-layouts  2.56 us
    pallas_call x2, Pallas kernels, products(): pl.pallas_call(functools.partial(products_kernel, transposed), out_shape=...  2.31 us

profile of v3, /device:TPU:1, one launch (start us, length us, event | category | flops | bytes accessed | tf_op | source)
XLA Modules:
  0.0 101.7 jit_solution(792675912422178770)
XLA Ops:
  0.6 0.0 copy-start.2
  0.6 0.0 copy-start.1
  1.3 0.0 copy-start
  1.3 1.2 %copy-done = bf16[4096,128]{1,0:T(8,128)(2,1)S(1)} copy-done((bf16[4096,128]{1,0:T(8,128)(2,1)S(1)}, bf16[4096,128]{1,0:T(8,128)(2,1)}, u32[]{:S(2)}) %copy-start) | copy-done | bytes 1048600
  2.5 20.5 %shard_map.72 = (bf16[2,4,4,256,128]{4,3,2,1,0:T(8,128)(2,1)S(1)}, bf16[32,256,256]{2,1,0:T(8,128)(2,1)S(1)}) custom-call(bf16[16,256,128]{2,1,0:T(8,128)(2,1)S(1)} %bitcast.5, bf16[32,256,256]{2,1,0:T(8,128)(2,1)} %bitcast.6), custom_call_target="tpu_custom_call" | custom-call | tf_op jit(solution)/shard_map/pallas_call | solution.py:145
  23.1 0.0 copy-done.2
  23.1 0.0 copy-done.1
  23.1 1.1 %shard_map.73.part = f32[16,256,128]{2,1,0:T(8,128)S(1)} custom-call(s32[1,1]{1,0:T(1,128)S(6)} %copy.19.count_ref, s32[1,1,32]{2,1,0:T(1,128)S(1)} %copy-done.1, s32[1,1,32]{2,1,0:T(1,128)S(1)} %copy-done.2, bf16[32,256,128]{2,1,0:T(8,128)(2,1)S(1)} %bitcast.4, bf16[32,256,256]{2,1,0:T(8,128)(2,1)S(1)} %get-tuple-element.18.tiles), custom_call_target="tpu_custom_call" | custom-call | tf_op jit(solution)/shard_map/pallas_call | solution.py:433
  24.3 27.9 %shard_map.74.panels = bf16[16,128,256]{2,1,0:T(8,128)(2,1)S(1)} custom-call(f32[16,256,128]{2,1,0:T(8,128)S(1)} %shard_map.73.part), custom_call_target="tpu_custom_call" | custom-call | tf_op jit(solution)/shard_map/pallas_call | solution.py:240
  52.2 1.2 %shard_map.75.part = f32[32,128,256]{2,1,0:T(8,128)S(1)} custom-call(s32[1,1]{1,0:T(1,128)S(6)} %copy.19.count_ref, s32[1,1,32]{2,1,0:T(1,128)S(1)} %copy-done.1, s32[1,1,32]{2,1,0:T(1,128)S(1)} %copy-done.2, bf16[16,128,256]{2,1,0:T(8,128)(2,1)S(1)} %shard_map.74.panels, bf16[32,256,256]{2,1,0:T(8,128)(2,1)S(1)} %get-tuple-element.18.tiles), custom_call_target="tpu_custom_call" | custom-call | tf_op jit(solution)/shard_map/pallas_call | solution.py:433
  53.3 45.8 %shard_map.76 = (f32[512,128]{1,0:T(8,128)S(1)}, f32[128,128]{1,0:T(8,128)S(1)}, f32[8,128]{1,0:T(8,128)S(1)}) custom-call(f32[32,128,256]{2,1,0:T(8,128)S(1)} %shard_map.75.part), custom_call_target="tpu_custom_call" | custom-call | tf_op jit(solution)/shard_map/pallas_call | solution.py:510
  99.1 0.5 slice.3
  100.3 0.7 copy.22
  101.0 0.6 copy.23
  (1 shorter events, 0.0 us)
Async XLA Ops:
  0.6 22.5 %copy-start.2 = (s32[1,1,32]{2,1,0:T(1,128)S(1)}, s32[1,1,32]{2,1,0:T(1,128)}, u32[]{:S(2)}) copy-start(s32[1,1,32]{2,1,0:T(1,128)} %col_ref.3) | copy-start | bytes 388
  0.6 22.5 %copy-start.1 = (s32[1,1,32]{2,1,0:T(1,128)S(1)}, s32[1,1,32]{2,1,0:T(1,128)}, u32[]{:S(2)}) copy-start(s32[1,1,32]{2,1,0:T(1,128)} %row_ref.3) | copy-start | bytes 388
  1.3 1.2 %copy-start = (bf16[4096,128]{1,0:T(8,128)(2,1)S(1)}, bf16[4096,128]{1,0:T(8,128)(2,1)}, u32[]{:S(2)}) copy-start(bf16[4096,128]{1,0:T(8,128)(2,1)} %param.7) | copy-start | bytes 3145732

commit v4 on v3

--- a/solution.py
+++ b/solution.py
@@ -9,6 +9,8 @@
 
 SUB = 8
 RING = 4
+TOP = 32000.0
+LEAST = 1e-33
 VMEM = pl.BlockSpec(memory_space=pltpu.VMEM)
 SMEM = pl.BlockSpec(memory_space=pltpu.SMEM)
 HBM = pl.BlockSpec(memory_space=pltpu.HBM)
@@ -46,13 +48,29 @@
             pltpu.make_async_copy(ref, ref, self.send).wait()
 
 
-def greet(peers):
+def announce(peers):
     barrier = pltpu.get_barrier_semaphore()
     for peer in peers:
         pl.semaphore_signal(
             barrier, inc=1, device_id=peer, device_id_type=pl.DeviceIdType.MESH
         )
-    pl.semaphore_wait(barrier, len(peers))
+
+
+def greet(peers):
+    announce(peers)
+    pl.semaphore_wait(pltpu.get_barrier_semaphore(), len(peers))
+
+
+def arrived(ref, sem):
+    pltpu.make_async_copy(ref, ref, sem).wait()
+
+
+def encode(value, inverse):
+    return jnp.round(value * inverse).astype(jnp.int32).astype(jnp.int16)
+
+
+def decode(code, unit):
+    return code.astype(jnp.int32).astype(jnp.float32) * unit
 
 
 def shifted(at, offset):
@@ -164,13 +182,15 @@
 IMAGE_COPIES = 24
 
 
-def image_kernel(part, image, sibling, total, relayed, merged, final, send, recv, send2):
+def image_kernel(
+    part, image, sibling, total, code, unit, got, units, send, recv, send2, send3
+):
     row, col = lax.axis_index("rows"), lax.axis_index("cols")
     x, core = col // 2, lax.rem(col, 2)
     twin = (row, x * 2 + 1 - core)
-    right, left = ((row, shifted(x, s) * 2 + core) for s in (1, 3))
+    peer = {o: (row, shifted(x, o) * 2 + core) for o in (1, 2, 3)}
     wires = Wires(send, recv)
-    greet([twin, right, left])
+    greet([twin, peer[1], peer[2], peer[3]])
     sub = image.shape[0] // 8
 
     def chunk(offset, which):
@@ -180,58 +200,47 @@
     swap = {
         o: wires.start(part.at[chunk(o, 1 - core)], sibling.at[o], twin) for o in order
     }
+    wires.send = send2
+    coded, scaled = {}, {}
     for o in order:
         swap[o].wait_recv()
-        total[o] = part[chunk(o, core)] + sibling[o]
-        if o == 2:
-            up = wires.start(total.at[2, 0], relayed.at[0], right)
-            down = wires.start(total.at[2, 1], relayed.at[1], left)
-        elif o == 1:
-            right_plain = wires.start(total.at[1, 1], final.at[0, 1], right)
-        elif o == 3:
-            left_plain = wires.start(total.at[3, 0], final.at[1, 0], left)
-    up.wait_recv()
-    merged[0] = total[1, 0] + relayed[0]
-    right_sum = wires.start(merged.at[0], final.at[0, 0], right)
-    down.wait_recv()
-    merged[1] = total[3, 1] + relayed[1]
-    left_sum = wires.start(merged.at[1], final.at[1, 1], left)
-
-    wires.send = send2
+        whole = part[chunk(o, core)] + sibling[o]
+        if o == 0:
+            total[...] = whole
+            continue
+        most = jnp.max(jnp.max(jnp.abs(whole), axis=0), axis=0, keepdims=True)
+        step = jnp.maximum(most, LEAST) * (1.0 / TOP)
+        unit[o - 1] = jnp.broadcast_to(step, unit.shape[1:])
+        code[o - 1] = encode(whole, (1.0 / step)[None])
+        coded[o] = wires.start(code.at[o - 1], got.at[o - 1], peer[o])
+        scaled[o] = wires.start(unit.at[o - 1], units.at[o - 1], peer[o])
+    for o in (1, 3, 2):
+        coded[o].wait_recv()
+        scaled[o].wait_recv()
+    wires.send = send3
     mine = (x * 2 + core) * sub
-    left_plain.wait_recv()
-    right_sum.wait_recv()
-    image[mine] = (total[0, 0] + (final[0, 0] + final[1, 0])).T.astype(image.dtype)
     sends = []
     for b in range(2):
-        if b == 1:
-            right_plain.wait_recv()
-            left_sum.wait_recv()
-            image[mine + 1] = (total[0, 1] + (final[0, 1] + final[1, 1])).T.astype(image.dtype)
+        value = total[b]
+        for o in (1, 2, 3):
+            value = value + decode(got[o - 1, b], units[o - 1, 0:1])
+        image[mine + b] = value.T.astype(image.dtype)
         block = image.at[mine + b]
-        sends.append([wires.start(block, block, peer) for peer in (right, left, twin)])
-    hops = []
-    for o, at, b_on, onward in ((3, 0, 0, right), (1, 1, 1, left)):
-        start = (shifted(x, o) * 2 + core) * sub
+        sends.append({o: wires.start(block, block, peer[o]) for o in (2, 1, 3)})
+    both = image.at[pl.ds(mine, sub)]
+    last = [wires.start(both, both, twin)]
+    for o in (1, 3, 2):
         for b in (0, 1):
-            sends[b][at].wait_recv()
-            block = image.at[start + b]
-            if b == b_on:
-                hops.append(wires.start(block, block, onward))
-        pair = image.at[pl.ds(start, sub)]
-        sends.append([wires.start(pair, pair, twin)])
-    far = (shifted(x, 2) * 2 + core) * sub
-    for b in (0, 1):
-        hops[b].wait_recv()
-        block = image.at[far + b]
-        sends.append([wires.start(block, block, twin)])
-    for b in (0, 1):
-        sends[b][2].wait_recv()
-    for copies in sends[2:]:
-        copies[0].wait_recv()
+            sends[b][o].wait_recv()
+        pair = image.at[pl.ds((shifted(x, RING - o) * 2 + core) * sub, sub)]
+        last.append(wires.start(pair, pair, twin))
+    for copy in last:
+        copy.wait_recv()
     wires.drain(image.at[pl.ds(0, 14)])
+    wires.send = send2
+    wires.drain(got, units)
     wires.send = send
-    wires.drain(part.at[pl.ds(0, 14)])
+    wires.drain(part.at[pl.ds(0, 8)])
 
 
 def sum_image(part):
@@ -244,12 +253,14 @@
         out_specs=VMEM,
         scratch_shapes=[
             pltpu.VMEM((RING, 2, width, depth), f32),
-            pltpu.VMEM((RING, 2, width, depth), f32),
             pltpu.VMEM((2, width, depth), f32),
-            pltpu.VMEM((2, width, depth), f32),
-            pltpu.VMEM((2, 2, width, depth), f32),
+            pltpu.VMEM((RING - 1, 2, width, depth), jnp.int16),
+            pltpu.VMEM((RING - 1, SUB, depth), f32),
+            pltpu.VMEM((RING - 1, 2, width, depth), jnp.int16),
+            pltpu.VMEM((RING - 1, SUB, depth), f32),
             pltpu.SemaphoreType.DMA,
             pltpu.SemaphoreType.DMA((IMAGE_COPIES,)),
+            pltpu.SemaphoreType.DMA,
             pltpu.SemaphoreType.DMA,
         ],
         compiler_params=pltpu.CompilerParams(
@@ -258,115 +269,128 @@
     )(part)
 
 
-SCATTER_COPIES = 36
-
-
-def scatter_sum(plane, wires, part, out, relayed, merged, final, total, hop, joined, close):
+SCATTER_STEPS = 14
+
+
+def tile_of(row):
+    return jnp.broadcast_to(row, (row.shape[1], row.shape[1])).T
+
+
+def scatter_sum(plane, wires, peers, part, out, code, got, line, lines, code2, got2, line2, lines2, own):
+    others = (2, 1, 3)
+    order = (2, 3, 1, 0)
+
     def block(h, first, second):
         return (h * RING + first) * RING + second
 
-    ups, downs = (2, 1), (3, 0)
-    ways = ((0, 1, ups, downs), (1, 3, downs, ups))
-    relay, flow = {}, {}
-    for h in (0, 1):
-        for way, step, onward, plain in ways:
-            for slot, s in enumerate(onward):
-                relay[h, way, slot] = wires.start(
-                    part.at[block(h, 2, s)], relayed.at[h, way, slot], plane.device(h, step, 0)
+    def column(tile):
+        return jnp.concatenate([tile, tile], axis=1)
+
+    announce(peers)
+    most = lax.fori_loop(
+        0,
+        part.shape[0],
+        lambda at, most: jnp.maximum(most, jnp.abs(part[at])),
+        jnp.zeros(part.shape[1:], jnp.float32),
+    )
+    most = jnp.broadcast_to(jnp.max(most, axis=1, keepdims=True), line.shape[1:] * 2)
+    unit = jnp.maximum(most, LEAST) * (1.0 / TOP)
+    line[...] = unit.T[:SUB]
+    inverse = column(1.0 / unit)
+    pl.semaphore_wait(pltpu.get_barrier_semaphore(), len(peers))
+    for h in (0, 1):
+        for o in others:
+            wires.start(line, lines.at[h, o - 1], plane.device(h, o, 0), h)
+    for at, s in enumerate(order):
+        for o in others:
+            for h in (0, 1):
+                code[h, s, o - 1] = encode(part[block(h, o, s)], inverse)
+                wires.start(
+                    code.at[h, s, o - 1], got.at[h, s, o - 1], plane.device(h, o, 0), 2 + 2 * at + h
                 )
-    for slot in (0, 1):
+    units, sums = {}, {}
+    for h in (0, 1):
+        arrived(lines.at[h], wires.recv.at[h])
+        units[h] = [tile_of(lines[h, k, 0:1]) for k in range(RING - 1)]
+        sums[h] = unit + (units[h][0] + units[h][1] + units[h][2])
+        line2[h] = line[...] + (lines[h, 0] + lines[h, 1] + lines[h, 2])
+        for s in others:
+            wires.start(line2.at[h], lines2.at[h, s - 1], plane.device(h, 0, s), 10 + h)
+    for at, s in enumerate(order):
         for h in (0, 1):
-            for way, step, onward, plain in ways:
-                s = plain[slot]
-                flow[h, way, s] = wires.start(
-                    part.at[block(h, step, s)], final.at[h, way, s], plane.device(h, step, 0)
+            arrived(got.at[h, s], wires.recv.at[2 + 2 * at + h])
+            total = part[block(h, 0, s)]
+            for k in range(RING - 1):
+                total = total + decode(got[h, s, k], column(units[h][k]))
+            if s == 0:
+                own[h] = total
+            else:
+                code2[h, s - 1] = encode(total, column(1.0 / sums[h]))
+                wires.start(
+                    code2.at[h, s - 1], got2.at[h, s - 1], plane.device(h, 0, s), 12 + h
                 )
-    for slot in (0, 1):
-        for h in (0, 1):
-            for way, step, onward, plain in ways:
-                s = onward[slot]
-                relay[h, way, slot].wait_recv()
-                merged[h, way, slot] = part[block(h, step, s)] + relayed[h, way, slot]
-                flow[h, way, s] = wires.start(
-                    merged.at[h, way, slot], final.at[h, way, s], plane.device(h, step, 0)
-                )
-    cut = out.shape[1] // 2
-    low, high = pl.ds(0, cut), pl.ds(cut, cut)
-    steps = ((0, 1, low, high), (1, 3, high, low))
-    near, direct, ended = {}, {}, {}
-    for s in (2, 3, 1, 0):
-        for h in (0, 1):
-            flow[h, 0, s].wait_recv()
-            flow[h, 1, s].wait_recv()
-            total[h, s] = part[block(h, 0, s)] + (final[h, 0, s] + final[h, 1, s])
-            for way, step, onward, plain in steps:
-                if s == 2:
-                    near[h, way] = wires.start(
-                        total.at[h, 2, onward], hop.at[h, way], plane.device(h, 0, step)
-                    )
-                elif s == step:
-                    direct[h, way] = wires.start(
-                        total.at[h, s, plain], close.at[h, way, plain], plane.device(h, 0, step)
-                    )
-    for h in (0, 1):
-        for way, step, onward, plain in steps:
-            near[h, way].wait_recv()
-            joined[h, way] = total[h, step, onward] + hop[h, way]
-            ended[h, way] = wires.start(
-                joined.at[h, way], close.at[h, way, onward], plane.device(h, 0, step)
-            )
-    for h in (0, 1):
-        for way in (0, 1):
-            direct[h, way].wait_recv()
-            ended[h, way].wait_recv()
-        out[h] = total[h, 0] + (close[h, 0] + close[h, 1])
+    for h in (0, 1):
+        arrived(lines2.at[h], wires.recv.at[10 + h])
+        arrived(got2.at[h], wires.recv.at[12 + h])
+        total = own[h]
+        for k in range(RING - 1):
+            total = total + decode(got2[h, k], column(tile_of(lines2[h, k, 0:1])))
+        out[h] = total
 
 
 def scatter_rooms(depth, width):
     f32 = jnp.float32
+    i16 = jnp.int16
+    others = RING - 1
     return [
-        pltpu.VMEM((2, 2, 2, depth, width), f32),
-        pltpu.VMEM((2, 2, 2, depth, width), f32),
-        pltpu.VMEM((2, 2, RING, depth, width), f32),
-        pltpu.VMEM((2, RING, depth, width), f32),
-        pltpu.VMEM((2, 2, depth // 2, width), f32),
-        pltpu.VMEM((2, 2, depth // 2, width), f32),
-        pltpu.VMEM((2, 2, depth, width), f32),
+        pltpu.VMEM((2, RING, others, depth, width), i16),
+        pltpu.VMEM((2, RING, others, depth, width), i16),
+        pltpu.VMEM((SUB, depth), f32),
+        pltpu.VMEM((2, others, SUB, depth), f32),
+        pltpu.VMEM((2, others, depth, width), i16),
+        pltpu.VMEM((2, others, depth, width), i16),
+        pltpu.VMEM((2, SUB, depth), f32),
+        pltpu.VMEM((2, others, SUB, depth), f32),
+        pltpu.VMEM((2, depth, width), f32),
     ]
 
 
 SQUARE_STEPS = 3
 
 
-def sum_square(wires, part, out, by_col, by_row, mine):
+def sum_square(wires, at, part, out, by_col, by_row, mine):
     rows, cols = lax.axis_size("rows"), lax.axis_size("cols")
     row, col = lax.axis_index("rows"), lax.axis_index("cols")
     share = part.shape[0] // cols
-    at = wires.used
-    wires.used += SQUARE_STEPS
+    x, core = col // 2, lax.rem(col, 2)
+    z, y = row // RING, lax.rem(row, RING)
 
     def span(at):
         return pl.ds(at * share, share)
 
-    def arrived(ref, step):
-        pltpu.make_async_copy(ref, ref, wires.recv.at[at + step]).wait()
-
-    for o in range(1, cols):
-        peer = lax.rem(col + o, cols)
+    far = {0: 0, 1: 1, 2: 2, 3: 1}
+    col_peers = [
+        shifted(x, o) * 2 + lax.rem(core + c, 2)
+        for o, c in ((2, 0), (2, 1), (1, 0), (3, 0), (1, 1), (3, 1), (0, 1))
+    ]
+    steps = [(a, b) for a in range(RING) for b in range(RING) if a or b]
+    row_peers = [
+        shifted(z, a) * RING + shifted(y, b)
+        for a, b in sorted(steps, key=lambda step: -far[step[0]] - far[step[1]])
+    ]
+    for peer in col_peers:
         wires.start(part.at[span(peer)], by_col.at[col], (row, peer), at)
     by_col[col] = part[span(col)]
-    arrived(by_col.at[pl.ds(0, cols - 1)], 0)
+    arrived(by_col.at[pl.ds(0, cols - 1)], wires.recv.at[at])
     mine[...] = jnp.sum(by_col[...], axis=0)
-    for o in range(1, rows):
-        wires.start(mine, by_row.at[row], (lax.rem(row + o, rows), col), at + 1)
+    for peer in row_peers:
+        wires.start(mine, by_row.at[row], (peer, col), at + 1)
     by_row[row] = mine[...]
-    arrived(by_row.at[pl.ds(0, rows - 1)], 1)
+    arrived(by_row.at[pl.ds(0, rows - 1)], wires.recv.at[at + 1])
     out[span(col)] = jnp.sum(by_row[...], axis=0)
-    for o in range(1, cols):
-        wires.start(
-            out.at[span(col)], out.at[span(col)], (row, lax.rem(col + o, cols)), at + 2
-        )
-    arrived(out.at[pl.ds(0, (cols - 1) * share)], 2)
+    for peer in col_peers:
+        wires.start(out.at[span(col)], out.at[span(col)], (row, peer), at + 2)
+    arrived(out.at[pl.ds(0, (cols - 1) * share)], wires.recv.at[at + 2])
     wires.drain(
         by_col.at[pl.ds(0, cols - 1)],
         by_row.at[pl.ds(0, rows - 1)],
@@ -477,14 +501,13 @@
 def basis_kernel(
     root, part, basis_ref, triangle_ref, spread_ref, x_ref, square, gram, inverse, *rest
 ):
-    rooms, (by_col, by_row, mine, send, recv, send2) = rest[:7], rest[7:]
+    rooms, (by_col, by_row, mine, send, recv, send2) = rest[:9], rest[9:]
     plane = Plane()
     wires = Wires(send, recv)
-    greet(all_peers())
-    scatter_sum(plane, wires, part, x_ref, *rooms)
+    scatter_sum(plane, wires, all_peers(), part, x_ref, *rooms)
     inner(x_ref, square)
     wires.send = send2
-    sum_square(wires, square, gram, by_col, by_row, mine)
+    sum_square(wires, SCATTER_STEPS, square, gram, by_col, by_row, mine)
     factor(gram[...], triangle_ref, inverse)
     width = x_ref.shape[2]
     for s in range(2):
@@ -497,9 +520,10 @@
     lengths = jnp.sum(jnp.where(diagonal, gram[...], 0.0), axis=0, keepdims=True)
     inverses = jnp.sum(inverse[...] * inverse[...], axis=0, keepdims=True)
     spread = jnp.sum(lengths * inverses, axis=1, keepdims=True)
-    spread_ref[...] = jnp.broadcast_to(spread, spread_ref.shape)
+    spread_ref[0, 0] = spread[0, 0]
     wires.send = send
-    wires.drain(part.at[pl.ds(0, 30)])
+    code, got, line, lines, code2, got2, line2, lines2, own = rooms
+    wires.drain(got, got2, lines, lines2)
 
 
 def orthonormalize(root, part):
@@ -512,17 +536,17 @@
         out_shape=[
             jax.ShapeDtypeStruct((2 * width, depth), f32),
             jax.ShapeDtypeStruct((depth, depth), f32),
-            jax.ShapeDtypeStruct((SUB, depth), f32),
+            jax.ShapeDtypeStruct((1, 1), f32),
         ],
         in_specs=[VMEM],
-        out_specs=[VMEM] * 3,
+        out_specs=[VMEM, VMEM, SMEM],
         scratch_shapes=[pltpu.VMEM((2, depth, width), f32)]
         + [square] * 3
         + scatter_rooms(depth, width)
         + square_rooms(depth, rows, cols)
         + [
             pltpu.SemaphoreType.DMA,
-            pltpu.SemaphoreType.DMA((SCATTER_COPIES + SQUARE_STEPS,)),
+            pltpu.SemaphoreType.DMA((SCATTER_STEPS + SQUARE_STEPS,)),
             pltpu.SemaphoreType.DMA,
         ],
         compiler_params=pltpu.CompilerParams(
@@ -539,7 +563,7 @@
     greet(all_peers())
     x[...] = basis_in[...].T / root
     square[...] = matmul(x[...], x[...], NT)
-    sum_square(wires, square, gram, by_col, by_row, mine)
+    sum_square(wires, 0, square, gram, by_col, by_row, mine)
     factor(gram[...], upper, inverse)
     basis_ref[...] = matmul(inverse[...], x[...], NN).T * root
     triangle_ref[...] = matmul(upper[...], triangle_in[...], NN)

time: 102 us -> 91.3 us (0.90)
  Pallas kernels: 96.5 us -> 86.3 us
    pallas_call x1, Pallas kernels: 45.8 us -> 37.7 us  [orthonormalize(): pl.pallas_call(functools.partial(basis_kernel, root), out_shape=[jax.Shap...]
    pallas_call x1, Pallas kernels: 27.9 us -> 25.7 us  [sum_image(): pl.pallas_call(image_kernel, out_shape=jax.ShapeDtypeStruct((blocks, dept...]
where the time goes in v4:
time: 91.3 us; the launch traced here: 91.1 us
  Pallas kernels  86.3 us (95%)
  local copies, waits for them, and re-layouts  2.56 us (3%)
  between operations  2.07 us (2%)
    pallas_call x1, Pallas kernels, orthonormalize(): pl.pallas_call(functools.partial(basis_kernel, root), out_shape=[jax.Shap...  37.7 us
    pallas_call x1, Pallas kernels, sum_image(): pl.pallas_call(image_kernel, out_shape=jax.ShapeDtypeStruct((blocks, dept...  25.7 us
    pallas_call x1, Pallas kernels, gather(): pl.pallas_call(gather_kernel, out_shape=[jax.ShapeDtypeStruct((2, rows //...  20.5 us
    unnamed x8, local copies, waits for them, and re-layouts  2.56 us
    pallas_call x2, Pallas kernels, products(): pl.pallas_call(functools.partial(products_kernel, transposed), out_shape=...  2.31 us

profile of v4, /device:TPU:1, one launch (start us, length us, event | category | flops | bytes accessed | tf_op | source)
XLA Modules:
  0.0 91.1 jit_solution(3586440253988753706)
XLA Ops:
  0.6 0.0 copy-start.2
  0.6 0.0 copy-start.1
  1.3 0.0 copy-start
  1.3 1.2 %copy-done = bf16[4096,128]{1,0:T(8,128)(2,1)S(1)} copy-done((bf16[4096,128]{1,0:T(8,128)(2,1)S(1)}, bf16[4096,128]{1,0:T(8,128)(2,1)}, u32[]{:S(2)}) %copy-start) | copy-done | bytes 1048600
  2.5 20.5 %shard_map.72 = (bf16[2,4,4,256,128]{4,3,2,1,0:T(8,128)(2,1)S(1)}, bf16[32,256,256]{2,1,0:T(8,128)(2,1)S(1)}) custom-call(bf16[16,256,128]{2,1,0:T(8,128)(2,1)S(1)} %bitcast.5, bf16[32,256,256]{2,1,0:T(8,128)(2,1)} %bitcast.6), custom_call_target="tpu_custom_call" | custom-call | tf_op jit(solution)/shard_map/pallas_call | solution.py:163
  23.1 0.0 copy-done.2
  23.1 0.0 copy-done.1
  23.1 1.1 %shard_map.73.part = f32[16,256,128]{2,1,0:T(8,128)S(1)} custom-call(s32[1,1]{1,0:T(1,128)S(6)} %copy.19.count_ref, s32[1,1,32]{2,1,0:T(1,128)S(1)} %copy-done.1, s32[1,1,32]{2,1,0:T(1,128)S(1)} %copy-done.2, bf16[32,256,128]{2,1,0:T(8,128)(2,1)S(1)} %bitcast.4, bf16[32,256,256]{2,1,0:T(8,128)(2,1)S(1)} %get-tuple-element.18.tiles), custom_call_target="tpu_custom_call" | custom-call | tf_op jit(solution)/shard_map/pallas_call | solution.py:457
  24.3 25.7 %shard_map.74.panels = bf16[16,128,256]{2,1,0:T(8,128)(2,1)S(1)} custom-call(f32[16,256,128]{2,1,0:T(8,128)S(1)} %shard_map.73.part), custom_call_target="tpu_custom_call" | custom-call | tf_op jit(solution)/shard_map/pallas_call | solution.py:249
  50.0 1.2 %shard_map.75.part = f32[32,128,256]{2,1,0:T(8,128)S(1)} custom-call(s32[1,1]{1,0:T(1,128)S(6)} %copy.19.count_ref, s32[1,1,32]{2,1,0:T(1,128)S(1)} %copy-done.1, s32[1,1,32]{2,1,0:T(1,128)S(1)} %copy-done.2, bf16[16,128,256]{2,1,0:T(8,128)(2,1)S(1)} %shard_map.74.panels, bf16[32,256,256]{2,1,0:T(8,128)(2,1)S(1)} %get-tuple-element.18.tiles), custom_call_target="tpu_custom_call" | custom-call | tf_op jit(solution)/shard_map/pallas_call | solution.py:457
  51.2 37.7 %shard_map.76 = (f32[512,128]{1,0:T(8,128)S(1)}, f32[128,128]{1,0:T(8,128)S(1)}, f32[1,1]{1,0:T(1,128)}) custom-call(f32[32,128,256]{2,1,0:T(8,128)S(1)} %shard_map.75.part), custom_call_target="tpu_custom_call" | custom-call | tf_op jit(solution)/shard_map/pallas_call | solution.py:534
  89.6 0.2 conditional.1
  89.8 0.7 copy.22
  90.5 0.6 copy.23
Async XLA Ops:
  0.6 22.5 %copy-start.2 = (s32[1,1,32]{2,1,0:T(1,128)S(1)}, s32[1,1,32]{2,1,0:T(1,128)}, u32[]{:S(2)}) copy-start(s32[1,1,32]{2,1,0:T(1,128)} %col_ref.3) | copy-start | bytes 388
  0.6 22.5 %copy-start.1 = (s32[1,1,32]{2,1,0:T(1,128)S(1)}, s32[1,1,32]{2,1,0:T(1,128)}, u32[]{:S(2)}) copy-start(s32[1,1,32]{2,1,0:T(1,128)} %row_ref.3) | copy-start | bytes 388
  1.3 1.2 %copy-start = (bf16[4096,128]{1,0:T(8,128)(2,1)S(1)}, bf16[4096,128]{1,0:T(8,128)(2,1)}, u32[]{:S(2)}) copy-start(bf16[4096,128]{1,0:T(8,128)(2,1)} %param.7) | copy-start | bytes 3145732

commit v5 on v4

--- a/solution.py
+++ b/solution.py
@@ -91,92 +91,84 @@
         return (self.row(half, first, second), self.col)
 
     def neighbours(self):
-        return [self.device(0, 1, 0), self.device(0, 3, 0), self.device(0, 0, 1), self.device(0, 0, 3)]
-
-
-GATHER_COPIES = 24
-
-
-def gather_kernel(basis, values, out, tiles, send, recv, local):
+        return [self.device(0, o, 0) for o in (2, 1, 3)] + [self.device(0, 0, o) for o in (2, 1, 3)]
+
+
+GATHER_COPIES = 36
+
+
+def gather_kernel(
+    basis, values, rows, cols, out, tiles, rows_out, cols_out, send, recv, local
+):
     plane = Plane()
     wires = Wires(send, recv)
     load = pltpu.make_async_copy(basis.at[pl.ds(plane.col * 2, 2)], out.at[:, 0, 0], local.at[0])
     load.start()
-    keep = pltpu.make_async_copy(values, tiles, local.at[1])
-    keep.start()
+    kept = [
+        pltpu.make_async_copy(src, dst, local.at[1 + at])
+        for at, (src, dst) in enumerate(
+            ((values, tiles), (rows, rows_out), (cols, cols_out))
+        )
+    ]
+    for copy in kept:
+        copy.start()
     greet(plane.neighbours())
     load.wait()
     cut = out.shape[3] // 2
     upper, lower = pl.ds(0, cut), pl.ds(cut, cut)
-    near, own, rest, relay, far, ends = {}, {}, {}, {}, {}, {}
-    for h in (0, 1):
-        src = out.at[h, 0, 0]
-        near[h] = [
-            wires.start(src, out.at[h, 3, 0], plane.device(h, 1, 0)),
-            wires.start(src, out.at[h, 1, 0], plane.device(h, 3, 0)),
-        ]
-    for h in (0, 1):
-        src = out.at[h, 0, 0]
-        own[h] = [
-            wires.start(src, out.at[h, 0, 3], plane.device(h, 0, 1)),
-            wires.start(src, out.at[h, 0, 1], plane.device(h, 0, 3)),
-        ]
-    for h in (0, 1):
-        near[h][0].wait_recv()
-        up = wires.start(out.at[h, 3, 0, upper], out.at[h, 2, 0, upper], plane.device(h, 1, 0))
-        near[h][1].wait_recv()
-        down = wires.start(out.at[h, 1, 0, lower], out.at[h, 2, 0, lower], plane.device(h, 3, 0))
-        relay[h] = [up, down]
-    for h in (0, 1):
-        own[h][0].wait_recv()
-        up = wires.start(out.at[h, 0, 3, upper], out.at[h, 0, 2, upper], plane.device(h, 0, 1))
-        own[h][1].wait_recv()
-        down = wires.start(out.at[h, 0, 1, lower], out.at[h, 0, 2, lower], plane.device(h, 0, 3))
-        far[h] = [up, down]
-    three = pl.ds(1, 3)
-    for h in (0, 1):
-        relay[h][0].wait_recv()
-        relay[h][1].wait_recv()
-        src = out.at[h, three, 0]
-        rest[h] = [
-            wires.start(src, out.at[h, three, 3], plane.device(h, 0, 1)),
-            wires.start(src, out.at[h, three, 1], plane.device(h, 0, 3)),
-        ]
-    for h in (0, 1):
-        rest[h][0].wait_recv()
-        up = wires.start(
-            out.at[h, three, 3, upper], out.at[h, three, 2, upper], plane.device(h, 0, 1)
-        )
-        rest[h][1].wait_recv()
-        down = wires.start(
-            out.at[h, three, 1, lower], out.at[h, three, 2, lower], plane.device(h, 0, 3)
-        )
-        ends[h] = [up, down]
-    for h in (0, 1):
-        for copy in far[h] + ends[h]:
-            copy.wait_recv()
-    keep.wait()
+    near, own, rest, ends = {}, {}, {}, []
+    for o in (1, 3, 2):
+        for h in (0, 1):
+            near[h, o] = wires.start(
+                out.at[h, 0, 0], out.at[h, RING - o, 0], plane.device(h, o, 0)
+            )
+    for o in (1, 3, 2):
+        for h in (0, 1):
+            own[h, o] = wires.start(
+                out.at[h, 0, 0], out.at[h, 0, RING - o], plane.device(h, 0, o)
+            )
+    for f in (3, 1, 2):
+        for h in (0, 1):
+            near[h, RING - f].wait_recv()
+            for o in (1, 3):
+                rest[h, f, o] = wires.start(
+                    out.at[h, f, 0], out.at[h, f, RING - o], plane.device(h, 0, o)
+                )
+    for f in (3, 1, 2):
+        for o, piece in ((1, upper), (3, lower)):
+            for h in (0, 1):
+                rest[h, f, o].wait_recv()
+                ends.append(
+                    wires.start(
+                        out.at[h, f, RING - o, piece], out.at[h, f, 2, piece], plane.device(h, 0, o)
+                    )
+                )
+    for copy in list(own.values()) + ends:
+        copy.wait_recv()
+    for copy in kept:
+        copy.wait()
     wires.drain(out.at[0], out.at[1, pl.ds(0, 3)], out.at[1, 3, pl.ds(0, 2)])
 
 
-def gather(basis, values, rows):
+def gather(basis, values, indices, rows):
     return pl.pallas_call(
         gather_kernel,
         out_shape=[
             jax.ShapeDtypeStruct((2, rows // RING, RING) + basis.shape[1:], basis.dtype),
             jax.ShapeDtypeStruct(values.shape, values.dtype),
-        ],
-        in_specs=[HBM, HBM],
-        out_specs=[VMEM, VMEM],
+        ]
+        + [jax.ShapeDtypeStruct(index.shape, index.dtype) for index in indices],
+        in_specs=[HBM] * 4,
+        out_specs=[VMEM] * 2 + [SMEM] * 2,
         scratch_shapes=[
             pltpu.SemaphoreType.DMA,
             pltpu.SemaphoreType.DMA((GATHER_COPIES,)),
-            pltpu.SemaphoreType.DMA((2,)),
+            pltpu.SemaphoreType.DMA((4,)),
         ],
         compiler_params=pltpu.CompilerParams(
             collective_id=0, has_side_effects=True, vmem_limit_bytes=44 << 20
         ),
-    )(basis, values)
+    )(basis, values, *indices)
 
 
 IMAGE_COPIES = 24
@@ -212,17 +204,19 @@
         step = jnp.maximum(most, LEAST) * (1.0 / TOP)
         unit[o - 1] = jnp.broadcast_to(step, unit.shape[1:])
         code[o - 1] = encode(whole, (1.0 / step)[None])
-        coded[o] = wires.start(code.at[o - 1], got.at[o - 1], peer[o])
         scaled[o] = wires.start(unit.at[o - 1], units.at[o - 1], peer[o])
+        coded[o, 0] = wires.start(code.at[o - 1, 0], got.at[o - 1, 0], peer[o])
+    for o in (2, 1, 3):
+        coded[o, 1] = wires.start(code.at[o - 1, 1], got.at[o - 1, 1], peer[o])
     for o in (1, 3, 2):
-        coded[o].wait_recv()
         scaled[o].wait_recv()
     wires.send = send3
     mine = (x * 2 + core) * sub
     sends = []
     for b in range(2):
         value = total[b]
-        for o in (1, 2, 3):
+        for o in (1, 3, 2):
+            coded[o, b].wait_recv()
             value = value + decode(got[o - 1, b], units[o - 1, 0:1])
         image[mine + b] = value.T.astype(image.dtype)
         block = image.at[mine + b]
@@ -457,7 +451,7 @@
     return pl.pallas_call(
         functools.partial(products_kernel, transposed),
         out_shape=jax.ShapeDtypeStruct(out_shape, jnp.float32),
-        in_specs=[SMEM, SMEM, SMEM, VMEM, VMEM],
+        in_specs=[VMEM, SMEM, SMEM, VMEM, VMEM],
         out_specs=VMEM,
         compiler_params=pltpu.CompilerParams(vmem_limit_bytes=32 << 20),
     )(count, rows, cols, panels, tiles)
@@ -596,23 +590,27 @@
     panel_blocks = start_basis.shape[0] // width
     rows, cols = lax.axis_size("rows"), lax.axis_size("cols")
     column_blocks = rows * panel_blocks // cols
-    basis_parts, tiles = gather(
-        start_basis.reshape(panel_blocks, width, depth),
-        block_values.reshape(block_values.shape[2:]),
-        rows,
-    )
+    held = [
+        pltpu.with_memory_space_constraint(array, pltpu.HBM)
+        for array in (
+            start_basis.reshape(panel_blocks, width, depth),
+            block_values.reshape(block_values.shape[2:]),
+            slot_row,
+            slot_col,
+        )
+    ]
+    basis_parts, tiles, *indices = gather(*held[:2], held[2:], rows)
     image_part = products(
         False,
         (panel_blocks, width, depth),
         slot_count,
-        slot_row,
-        slot_col,
+        *indices,
         basis_parts.reshape(column_blocks, width, depth),
         tiles,
     )
     image = sum_image(image_part)
     back_part = products(
-        True, (column_blocks, depth, width), slot_count, slot_row, slot_col, image, tiles
+        True, (column_blocks, depth, width), slot_count, *indices, image, tiles
     )
     root = float(rows * panel_blocks * width) ** 0.5
     basis, triangle, spread = orthonormalize(root, back_part)

time: 91.3 us -> 87.7 us (0.961)
  Pallas kernels: 86.3 us -> 84.1 us
  local copies, waits for them, and re-layouts: 2.56 us -> 1.33 us
    pallas_call x1, Pallas kernels: 25.7 us -> 21.5 us  [sum_image(): pl.pallas_call(image_kernel, out_shape=jax.ShapeDtypeStruct((blocks, dept...]
    unnamed x8 -> x2, local copies, waits for them, and re-layouts: 2.56 us -> 1.33 us
where the time goes in v5:
time: 87.7 us; the launch traced here: 87.6 us
  Pallas kernels  84.1 us (96%)
  between operations  1.93 us (2%)
  local copies, waits for them, and re-layouts  1.33 us (2%)
    pallas_call x1, Pallas kernels, orthonormalize(): pl.pallas_call(functools.partial(basis_kernel, root), out_shape=[jax.Shap...  38.4 us
    pallas_call x1, Pallas kernels, sum_image(): pl.pallas_call(image_kernel, out_shape=jax.ShapeDtypeStruct((blocks, dept...  21.5 us
    pallas_call x1, Pallas kernels, gather(): pl.pallas_call(gather_kernel, out_shape=[jax.ShapeDtypeStruct((2, rows //...  21.1 us
    pallas_call x2, Pallas kernels, products(): pl.pallas_call(functools.partial(products_kernel, transposed), out_shape=...  3.13 us

profile of v5, /device:TPU:1, one launch (start us, length us, event | category | flops | bytes accessed | tf_op | source)
XLA Modules:
  0.0 87.6 jit_solution(13777037933183527532)
XLA Ops:
  1.3 21.1 %shard_map.72 = (bf16[2,4,4,256,128]{4,3,2,1,0:T(8,128)(2,1)S(1)}, bf16[32,256,256]{2,1,0:T(8,128)(2,1)S(1)}, s32[1,1,32]{2,1,0:T(1,128)S(1)}, s32[1,1,32]{2,1,0:T(1,128)S(1)}) custom-call(bf16[16,256,128]{2,1,0:T(8,128)(2,1)} %bitcast.6, bf16[32,256,256]{2,1,0:T(8,128)(2,1)} %bitcast.5, s32[1,1,32]{2,1,0:T(1,128)} %rows.1, s32[1,1,32]{2,1,0:T(1,128)} %cols.1), custom_call_target="tpu_custom_call" | custom-call | tf_op jit(solution)/shard_map/pallas_call | solution.py:154
  22.3 1.6 %shard_map.73.part = f32[16,256,128]{2,1,0:T(8,128)S(1)} custom-call(s32[1,1]{1,0:T(1,128)S(6)} %copy.19.count_ref, s32[1,1,32]{2,1,0:T(1,128)S(1)} %get-tuple-element.19.row_ref, s32[1,1,32]{2,1,0:T(1,128)S(1)} %get-tuple-element.20.col_ref, bf16[32,256,128]{2,1,0:T(8,128)(2,1)S(1)} %bitcast.4, bf16[32,256,256]{2,1,0:T(8,128)(2,1)S(1)} %get-tuple-element.22.tiles), custom_call_target="tpu_custom_call" | custom-call | tf_op jit(solution)/shard_map/pallas_call | solution.py:451
  24.0 21.5 %shard_map.74.panels = bf16[16,128,256]{2,1,0:T(8,128)(2,1)S(1)} custom-call(f32[16,256,128]{2,1,0:T(8,128)S(1)} %shard_map.73.part), custom_call_target="tpu_custom_call" | custom-call | tf_op jit(solution)/shard_map/pallas_call | solution.py:243
  45.5 1.5 %shard_map.75.part = f32[32,128,256]{2,1,0:T(8,128)S(1)} custom-call(s32[1,1]{1,0:T(1,128)S(6)} %copy.19.count_ref, s32[1,1,32]{2,1,0:T(1,128)S(1)} %get-tuple-element.19.row_ref, s32[1,1,32]{2,1,0:T(1,128)S(1)} %get-tuple-element.20.col_ref, bf16[16,128,256]{2,1,0:T(8,128)(2,1)S(1)} %shard_map.74.panels, bf16[32,256,256]{2,1,0:T(8,128)(2,1)S(1)} %get-tuple-element.22.tiles), custom_call_target="tpu_custom_call" | custom-call | tf_op jit(solution)/shard_map/pallas_call | solution.py:451
  47.0 38.4 %shard_map.76 = (f32[512,128]{1,0:T(8,128)S(1)}, f32[128,128]{1,0:T(8,128)S(1)}, f32[1,1]{1,0:T(1,128)}) custom-call(f32[32,128,256]{2,1,0:T(8,128)S(1)} %shard_map.75.part), custom_call_target="tpu_custom_call" | custom-call | tf_op jit(solution)/shard_map/pallas_call | solution.py:528
  86.0 0.2 conditional.1
  86.2 0.7 copy.22
  86.9 0.6 copy.23

commit v6 on v5

--- a/solution.py
+++ b/solution.py
@@ -94,7 +94,7 @@
         return [self.device(0, o, 0) for o in (2, 1, 3)] + [self.device(0, 0, o) for o in (2, 1, 3)]
 
 
-GATHER_COPIES = 36
+GATHER_COPIES = 38
 
 
 def gather_kernel(
@@ -116,15 +116,15 @@
     load.wait()
     cut = out.shape[3] // 2
     upper, lower = pl.ds(0, cut), pl.ds(cut, cut)
-    near, own, rest, ends = {}, {}, {}, []
+    near, rest, ends = {}, {}, []
     for o in (1, 3, 2):
         for h in (0, 1):
             near[h, o] = wires.start(
                 out.at[h, 0, 0], out.at[h, RING - o, 0], plane.device(h, o, 0)
             )
-    for o in (1, 3, 2):
+    for o in (1, 3):
         for h in (0, 1):
-            own[h, o] = wires.start(
+            rest[h, 0, o] = wires.start(
                 out.at[h, 0, 0], out.at[h, 0, RING - o], plane.device(h, 0, o)
             )
     for f in (3, 1, 2):
@@ -134,7 +134,7 @@
                 rest[h, f, o] = wires.start(
                     out.at[h, f, 0], out.at[h, f, RING - o], plane.device(h, 0, o)
                 )
-    for f in (3, 1, 2):
+    for f in (0, 3, 1, 2):
         for o, piece in ((1, upper), (3, lower)):
             for h in (0, 1):
                 rest[h, f, o].wait_recv()
@@ -143,7 +143,7 @@
                         out.at[h, f, RING - o, piece], out.at[h, f, 2, piece], plane.device(h, 0, o)
                     )
                 )
-    for copy in list(own.values()) + ends:
+    for copy in ends:
         copy.wait_recv()
     for copy in kept:
         copy.wait()
@@ -292,10 +292,11 @@
     line[...] = unit.T[:SUB]
     inverse = column(1.0 / unit)
     pl.semaphore_wait(pltpu.get_barrier_semaphore(), len(peers))
-    for h in (0, 1):
-        for o in others:
-            wires.start(line, lines.at[h, o - 1], plane.device(h, o, 0), h)
     for at, s in enumerate(order):
+        if at == 1:
+            for h in (0, 1):
+                for o in others:
+                    wires.start(line, lines.at[h, o - 1], plane.device(h, o, 0), h)
         for o in others:
             for h in (0, 1):
                 code[h, s, o - 1] = encode(part[block(h, o, s)], inverse)
@@ -409,7 +410,7 @@
     ]
 
 
-GROUP = 8
+GROUP = 16
 
 
 def local_column(column):
@@ -498,7 +499,11 @@
     rooms, (by_col, by_row, mine, send, recv, send2) = rest[:9], rest[9:]
     plane = Plane()
     wires = Wires(send, recv)
-    scatter_sum(plane, wires, all_peers(), part, x_ref, *rooms)
+    row, cols = lax.axis_index("rows"), lax.axis_size("cols")
+    peers = plane.neighbours() + [
+        (row, lax.rem(plane.col + o, cols)) for o in range(1, cols)
+    ]
+    scatter_sum(plane, wires, peers, part, x_ref, *rooms)
     inner(x_ref, square)
     wires.send = send2
     sum_square(wires, SCATTER_STEPS, square, gram, by_col, by_row, mine)

time: 87.7 us -> 85.7 us (0.977)
  Pallas kernels: 84.1 us -> 82.1 us
    pallas_call x1, Pallas kernels: 21.1 us -> 19.8 us  [gather(): pl.pallas_call(gather_kernel, out_shape=[jax.ShapeDtypeStruct((2, rows //...]
where the time goes in v6:
time: 85.7 us; the launch traced here: 85.6 us
  Pallas kernels  82.1 us (96%)
  between operations  1.93 us (2%)
  local copies, waits for them, and re-layouts  1.33 us (2%)
    pallas_call x1, Pallas kernels, orthonormalize(): pl.pallas_call(functools.partial(basis_kernel, root), out_shape=[jax.Shap...  37.7 us
    pallas_call x1, Pallas kernels, sum_image(): pl.pallas_call(image_kernel, out_shape=jax.ShapeDtypeStruct((blocks, dept...  21.8 us
    pallas_call x1, Pallas kernels, gather(): pl.pallas_call(gather_kernel, out_shape=[jax.ShapeDtypeStruct((2, rows //...  19.8 us
    pallas_call x2, Pallas kernels, products(): pl.pallas_call(functools.partial(products_kernel, transposed), out_shape=...  2.84 us

profile of v6, /device:TPU:1, one launch (start us, length us, event | category | flops | bytes accessed | tf_op | source)
XLA Modules:
  0.0 85.6 jit_solution(10838729498494299462)
XLA Ops:
  1.3 19.8 %shard_map.72 = (bf16[2,4,4,256,128]{4,3,2,1,0:T(8,128)(2,1)S(1)}, bf16[32,256,256]{2,1,0:T(8,128)(2,1)S(1)}, s32[1,1,32]{2,1,0:T(1,128)S(1)}, s32[1,1,32]{2,1,0:T(1,128)S(1)}) custom-call(bf16[16,256,128]{2,1,0:T(8,128)(2,1)} %bitcast.6, bf16[32,256,256]{2,1,0:T(8,128)(2,1)} %bitcast.5, s32[1,1,32]{2,1,0:T(1,128)} %rows.1, s32[1,1,32]{2,1,0:T(1,128)} %cols.1), custom_call_target="tpu_custom_call" | custom-call | tf_op jit(solution)/shard_map/pallas_call | solution.py:154
  21.1 1.4 %shard_map.73.part = f32[16,256,128]{2,1,0:T(8,128)S(1)} custom-call(s32[1,1]{1,0:T(1,128)S(6)} %copy.19.count_ref, s32[1,1,32]{2,1,0:T(1,128)S(1)} %get-tuple-element.19.row_ref, s32[1,1,32]{2,1,0:T(1,128)S(1)} %get-tuple-element.20.col_ref, bf16[32,256,128]{2,1,0:T(8,128)(2,1)S(1)} %bitcast.4, bf16[32,256,256]{2,1,0:T(8,128)(2,1)S(1)} %get-tuple-element.22.tiles), custom_call_target="tpu_custom_call" | custom-call | tf_op jit(solution)/shard_map/pallas_call | solution.py:452
  22.5 21.8 %shard_map.74.panels = bf16[16,128,256]{2,1,0:T(8,128)(2,1)S(1)} custom-call(f32[16,256,128]{2,1,0:T(8,128)S(1)} %shard_map.73.part), custom_call_target="tpu_custom_call" | custom-call | tf_op jit(solution)/shard_map/pallas_call | solution.py:243
  44.3 1.4 %shard_map.75.part = f32[32,128,256]{2,1,0:T(8,128)S(1)} custom-call(s32[1,1]{1,0:T(1,128)S(6)} %copy.19.count_ref, s32[1,1,32]{2,1,0:T(1,128)S(1)} %get-tuple-element.19.row_ref, s32[1,1,32]{2,1,0:T(1,128)S(1)} %get-tuple-element.20.col_ref, bf16[16,128,256]{2,1,0:T(8,128)(2,1)S(1)} %shard_map.74.panels, bf16[32,256,256]{2,1,0:T(8,128)(2,1)S(1)} %get-tuple-element.22.tiles), custom_call_target="tpu_custom_call" | custom-call | tf_op jit(solution)/shard_map/pallas_call | solution.py:452
  45.8 37.7 %shard_map.76 = (f32[512,128]{1,0:T(8,128)S(1)}, f32[128,128]{1,0:T(8,128)S(1)}, f32[1,1]{1,0:T(1,128)}) custom-call(f32[32,128,256]{2,1,0:T(8,128)S(1)} %shard_map.75.part), custom_call_target="tpu_custom_call" | custom-call | tf_op jit(solution)/shard_map/pallas_call | solution.py:533
  84.0 0.2 conditional.1
  84.2 0.7 copy.22
  85.0 0.6 copy.23

commit v7 on v6

--- a/solution.py
+++ b/solution.py
@@ -263,14 +263,14 @@
     )(part)
 
 
-SCATTER_STEPS = 14
+SCATTER_STEPS = 22
 
 
 def tile_of(row):
     return jnp.broadcast_to(row, (row.shape[1], row.shape[1])).T
 
 
-def scatter_sum(plane, wires, peers, part, out, code, got, line, lines, code2, got2, line2, lines2, own):
+def scatter_sum(plane, wires, peers, part, out, early, hop, code, got, line, lines, code2, got2, line2, lines2, own):
     others = (2, 1, 3)
     order = (2, 3, 1, 0)
 
@@ -292,17 +292,24 @@
     line[...] = unit.T[:SUB]
     inverse = column(1.0 / unit)
     pl.semaphore_wait(pltpu.get_barrier_semaphore(), len(peers))
+    for h in (0, 1):
+        for o in others:
+            wires.start(line, lines.at[h, o - 1], plane.device(h, o, 0), h)
+    way = {2: 0, 1: 0, 3: 1, 0: 1}
+    offset = (1, 3)
     for at, s in enumerate(order):
-        if at == 1:
-            for h in (0, 1):
-                for o in others:
-                    wires.start(line, lines.at[h, o - 1], plane.device(h, o, 0), h)
-        for o in others:
-            for h in (0, 1):
-                code[h, s, o - 1] = encode(part[block(h, o, s)], inverse)
-                wires.start(
-                    code.at[h, s, o - 1], got.at[h, s, o - 1], plane.device(h, o, 0), 2 + 2 * at + h
-                )
+        for h in (0, 1):
+            early[h, s] = encode(part[block(h, 2, s)], inverse)
+            wires.start(
+                early.at[h, s], hop.at[h, s], plane.device(h, offset[way[s]], 0), 14 + 2 * at + h
+            )
+    for at, s in enumerate(order):
+        w = 1 - way[s]
+        for h in (0, 1):
+            code[h, s, w] = encode(part[block(h, offset[w], s)], inverse)
+            wires.start(
+                code.at[h, s, w], got.at[h, s, w], plane.device(h, offset[w], 0), 2 + 2 * at + h
+            )
     units, sums = {}, {}
     for h in (0, 1):
         arrived(lines.at[h], wires.recv.at[h])
@@ -312,11 +319,22 @@
         for s in others:
             wires.start(line2.at[h], lines2.at[h, s - 1], plane.device(h, 0, s), 10 + h)
     for at, s in enumerate(order):
+        w = way[s]
+        for h in (0, 1):
+            near = units[h][offset[w] - 1]
+            arrived(hop.at[h, s], wires.recv.at[14 + 2 * at + h])
+            merged = part[block(h, offset[w], s)] + decode(hop[h, s], column(near))
+            code[h, s, w] = encode(merged, column(1.0 / (unit + near)))
+            wires.start(
+                code.at[h, s, w], got.at[h, s, w], plane.device(h, offset[w], 0), 2 + 2 * at + h
+            )
+    for at, s in enumerate(order):
+        w = way[s]
         for h in (0, 1):
             arrived(got.at[h, s], wires.recv.at[2 + 2 * at + h])
-            total = part[block(h, 0, s)]
-            for k in range(RING - 1):
-                total = total + decode(got[h, s, k], column(units[h][k]))
+            both = units[h][offset[w] - 1] + units[h][1]
+            total = part[block(h, 0, s)] + decode(got[h, s, w], column(both))
+            total = total + decode(got[h, s, 1 - w], column(units[h][offset[1 - w] - 1]))
             if s == 0:
                 own[h] = total
             else:
@@ -338,8 +356,10 @@
     i16 = jnp.int16
     others = RING - 1
     return [
-        pltpu.VMEM((2, RING, others, depth, width), i16),
-        pltpu.VMEM((2, RING, others, depth, width), i16),
+        pltpu.VMEM((2, RING, depth, width), i16),
+        pltpu.VMEM((2, RING, depth, width), i16),
+        pltpu.VMEM((2, RING, 2, depth, width), i16),
+        pltpu.VMEM((2, RING, 2, depth, width), i16),
         pltpu.VMEM((SUB, depth), f32),
         pltpu.VMEM((2, others, SUB, depth), f32),
         pltpu.VMEM((2, others, depth, width), i16),
@@ -496,7 +516,7 @@
 def basis_kernel(
     root, part, basis_ref, triangle_ref, spread_ref, x_ref, square, gram, inverse, *rest
 ):
-    rooms, (by_col, by_row, mine, send, recv, send2) = rest[:9], rest[9:]
+    rooms, (by_col, by_row, mine, send, recv, send2) = rest[:11], rest[11:]
     plane = Plane()
     wires = Wires(send, recv)
     row, cols = lax.axis_index("rows"), lax.axis_size("cols")
@@ -521,8 +541,8 @@
     spread = jnp.sum(lengths * inverses, axis=1, keepdims=True)
     spread_ref[0, 0] = spread[0, 0]
     wires.send = send
-    code, got, line, lines, code2, got2, line2, lines2, own = rooms
-    wires.drain(got, got2, lines, lines2)
+    early, hop, code, got, line, lines, code2, got2, line2, lines2, own = rooms
+    wires.drain(hop, got, got2, lines, lines2)
 
 
 def orthonormalize(root, part):

time: 85.7 us -> 83.8 us (0.978)
  Pallas kernels: 82.1 us -> 80.2 us
    pallas_call x1, Pallas kernels: 37.7 us -> 35.7 us  [orthonormalize(): pl.pallas_call(functools.partial(basis_kernel, root), out_shape=[jax.Shap...]
where the time goes in v7:
time: 83.8 us; the launch traced here: 83.6 us
  Pallas kernels  80.2 us (96%)
  between operations  1.93 us (2%)
  local copies, waits for them, and re-layouts  1.33 us (2%)
    pallas_call x1, Pallas kernels, orthonormalize(): pl.pallas_call(functools.partial(basis_kernel, root), out_shape=[jax.Shap...  35.7 us
    pallas_call x1, Pallas kernels, sum_image(): pl.pallas_call(image_kernel, out_shape=jax.ShapeDtypeStruct((blocks, dept...  21.8 us
    pallas_call x1, Pallas kernels, gather(): pl.pallas_call(gather_kernel, out_shape=[jax.ShapeDtypeStruct((2, rows //...  19.8 us
    pallas_call x2, Pallas kernels, products(): pl.pallas_call(functools.partial(products_kernel, transposed), out_shape=...  2.84 us

profile of v7, /device:TPU:1, one launch (start us, length us, event | category | flops | bytes accessed | tf_op | source)
XLA Modules:
  0.0 83.6 jit_solution(17990519410640790732)
XLA Ops:
  1.3 19.8 %shard_map.72 = (bf16[2,4,4,256,128]{4,3,2,1,0:T(8,128)(2,1)S(1)}, bf16[32,256,256]{2,1,0:T(8,128)(2,1)S(1)}, s32[1,1,32]{2,1,0:T(1,128)S(1)}, s32[1,1,32]{2,1,0:T(1,128)S(1)}) custom-call(bf16[16,256,128]{2,1,0:T(8,128)(2,1)} %bitcast.6, bf16[32,256,256]{2,1,0:T(8,128)(2,1)} %bitcast.5, s32[1,1,32]{2,1,0:T(1,128)} %rows.1, s32[1,1,32]{2,1,0:T(1,128)} %cols.1), custom_call_target="tpu_custom_call" | custom-call | tf_op jit(solution)/shard_map/pallas_call | solution.py:154
  21.1 1.4 %shard_map.73.part = f32[16,256,128]{2,1,0:T(8,128)S(1)} custom-call(s32[1,1]{1,0:T(1,128)S(6)} %copy.19.count_ref, s32[1,1,32]{2,1,0:T(1,128)S(1)} %get-tuple-element.19.row_ref, s32[1,1,32]{2,1,0:T(1,128)S(1)} %get-tuple-element.20.col_ref, bf16[32,256,128]{2,1,0:T(8,128)(2,1)S(1)} %bitcast.4, bf16[32,256,256]{2,1,0:T(8,128)(2,1)S(1)} %get-tuple-element.22.tiles), custom_call_target="tpu_custom_call" | custom-call | tf_op jit(solution)/shard_map/pallas_call | solution.py:472
  22.5 21.8 %shard_map.74.panels = bf16[16,128,256]{2,1,0:T(8,128)(2,1)S(1)} custom-call(f32[16,256,128]{2,1,0:T(8,128)S(1)} %shard_map.73.part), custom_call_target="tpu_custom_call" | custom-call | tf_op jit(solution)/shard_map/pallas_call | solution.py:243
  44.3 1.4 %shard_map.75.part = f32[32,128,256]{2,1,0:T(8,128)S(1)} custom-call(s32[1,1]{1,0:T(1,128)S(6)} %copy.19.count_ref, s32[1,1,32]{2,1,0:T(1,128)S(1)} %get-tuple-element.19.row_ref, s32[1,1,32]{2,1,0:T(1,128)S(1)} %get-tuple-element.20.col_ref, bf16[16,128,256]{2,1,0:T(8,128)(2,1)S(1)} %shard_map.74.panels, bf16[32,256,256]{2,1,0:T(8,128)(2,1)S(1)} %get-tuple-element.22.tiles), custom_call_target="tpu_custom_call" | custom-call | tf_op jit(solution)/shard_map/pallas_call | solution.py:472
  45.8 35.7 %shard_map.76 = (f32[512,128]{1,0:T(8,128)S(1)}, f32[128,128]{1,0:T(8,128)S(1)}, f32[1,1]{1,0:T(1,128)}) custom-call(f32[32,128,256]{2,1,0:T(8,128)S(1)} %shard_map.75.part), custom_call_target="tpu_custom_call" | custom-call | tf_op jit(solution)/shard_map/pallas_call | solution.py:553
  82.1 0.2 conditional.1
  82.3 0.7 copy.22
  83.0 0.6 copy.23

commit v8 on v7

--- a/solution.py
+++ b/solution.py
@@ -342,12 +342,15 @@
                 wires.start(
                     code2.at[h, s - 1], got2.at[h, s - 1], plane.device(h, 0, s), 12 + h
                 )
+    last = {}
     for h in (0, 1):
         arrived(lines2.at[h], wires.recv.at[10 + h])
+        last[h] = [tile_of(lines2[h, k, 0:1]) for k in range(RING - 1)]
+    for h in (0, 1):
         arrived(got2.at[h], wires.recv.at[12 + h])
         total = own[h]
         for k in range(RING - 1):
-            total = total + decode(got2[h, k], column(tile_of(lines2[h, k, 0:1])))
+            total = total + decode(got2[h, k], column(last[h][k]))
         out[h] = total
 
 
@@ -497,7 +500,7 @@
         for k in range(SUB):
             pivot = columns[k][k : k + 1, :]
             pivots = jnp.where(top == k, pivot, pivots)
-            ratio = jnp.where(position > k, columns[k] * (1.0 / pivot), 0.0)
+            ratio = jnp.where(position > k, columns[k], 0.0) * (1.0 / pivot)
             lead = lead - ratio * lead[k : k + 1, :]
             tail = tail - ratio * tail[k : k + 1, :]
             for j in range(k + 1, SUB):

time: 83.8 us -> 83.5 us (level)
  no operation moved by 1% of the time
where the time goes in v8:
time: 83.5 us; the launch traced here: 83.4 us
  Pallas kernels  79.9 us (96%)
  between operations  1.93 us (2%)
  local copies, waits for them, and re-layouts  1.33 us (2%)
    pallas_call x1, Pallas kernels, orthonormalize(): pl.pallas_call(functools.partial(basis_kernel, root), out_shape=[jax.Shap...  35.4 us
    pallas_call x1, Pallas kernels, sum_image(): pl.pallas_call(image_kernel, out_shape=jax.ShapeDtypeStruct((blocks, dept...  21.8 us
    pallas_call x1, Pallas kernels, gather(): pl.pallas_call(gather_kernel, out_shape=[jax.ShapeDtypeStruct((2, rows //...  19.8 us
    pallas_call x2, Pallas kernels, products(): pl.pallas_call(functools.partial(products_kernel, transposed), out_shape=...  2.84 us

profile of v8, /device:TPU:1, one launch (start us, length us, event | category | flops | bytes accessed | tf_op | source)
XLA Modules:
  0.0 83.4 jit_solution(12421252295842518032)
XLA Ops:
  1.3 19.8 %shard_map.72 = (bf16[2,4,4,256,128]{4,3,2,1,0:T(8,128)(2,1)S(1)}, bf16[32,256,256]{2,1,0:T(8,128)(2,1)S(1)}, s32[1,1,32]{2,1,0:T(1,128)S(1)}, s32[1,1,32]{2,1,0:T(1,128)S(1)}) custom-call(bf16[16,256,128]{2,1,0:T(8,128)(2,1)} %bitcast.6, bf16[32,256,256]{2,1,0:T(8,128)(2,1)} %bitcast.5, s32[1,1,32]{2,1,0:T(1,128)} %rows.1, s32[1,1,32]{2,1,0:T(1,128)} %cols.1), custom_call_target="tpu_custom_call" | custom-call | tf_op jit(solution)/shard_map/pallas_call | solution.py:154
  21.1 1.4 %shard_map.73.part = f32[16,256,128]{2,1,0:T(8,128)S(1)} custom-call(s32[1,1]{1,0:T(1,128)S(6)} %copy.19.count_ref, s32[1,1,32]{2,1,0:T(1,128)S(1)} %get-tuple-element.19.row_ref, s32[1,1,32]{2,1,0:T(1,128)S(1)} %get-tuple-element.20.col_ref, bf16[32,256,128]{2,1,0:T(8,128)(2,1)S(1)} %bitcast.4, bf16[32,256,256]{2,1,0:T(8,128)(2,1)S(1)} %get-tuple-element.22.tiles), custom_call_target="tpu_custom_call" | custom-call | tf_op jit(solution)/shard_map/pallas_call | solution.py:475
  22.5 21.8 %shard_map.74.panels = bf16[16,128,256]{2,1,0:T(8,128)(2,1)S(1)} custom-call(f32[16,256,128]{2,1,0:T(8,128)S(1)} %shard_map.73.part), custom_call_target="tpu_custom_call" | custom-call | tf_op jit(solution)/shard_map/pallas_call | solution.py:243
  44.3 1.4 %shard_map.75.part = f32[32,128,256]{2,1,0:T(8,128)S(1)} custom-call(s32[1,1]{1,0:T(1,128)S(6)} %copy.19.count_ref, s32[1,1,32]{2,1,0:T(1,128)S(1)} %get-tuple-element.19.row_ref, s32[1,1,32]{2,1,0:T(1,128)S(1)} %get-tuple-element.20.col_ref, bf16[16,128,256]{2,1,0:T(8,128)(2,1)S(1)} %shard_map.74.panels, bf16[32,256,256]{2,1,0:T(8,128)(2,1)S(1)} %get-tuple-element.22.tiles), custom_call_target="tpu_custom_call" | custom-call | tf_op jit(solution)/shard_map/pallas_call | solution.py:475
  45.8 35.4 %shard_map.76 = (f32[512,128]{1,0:T(8,128)S(1)}, f32[128,128]{1,0:T(8,128)S(1)}, f32[1,1]{1,0:T(1,128)}) custom-call(f32[32,128,256]{2,1,0:T(8,128)S(1)} %shard_map.75.part), custom_call_target="tpu_custom_call" | custom-call | tf_op jit(solution)/shard_map/pallas_call | solution.py:556
  81.8 0.2 conditional.1
  82.0 0.7 copy.22
  82.7 0.6 copy.23

commit v9 on v7

--- a/solution.py
+++ b/solution.py
@@ -194,20 +194,21 @@
     }
     wires.send = send2
     coded, scaled = {}, {}
-    for o in order:
+    for o in order[:3]:
         swap[o].wait_recv()
         whole = part[chunk(o, core)] + sibling[o]
-        if o == 0:
-            total[...] = whole
-            continue
         most = jnp.max(jnp.max(jnp.abs(whole), axis=0), axis=0, keepdims=True)
         step = jnp.maximum(most, LEAST) * (1.0 / TOP)
+        inverse = 1.0 / step
+        code[o - 1, 0] = encode(whole[0], inverse)
+        coded[o, 0] = wires.start(code.at[o - 1, 0], got.at[o - 1, 0], peer[o])
         unit[o - 1] = jnp.broadcast_to(step, unit.shape[1:])
-        code[o - 1] = encode(whole, (1.0 / step)[None])
         scaled[o] = wires.start(unit.at[o - 1], units.at[o - 1], peer[o])
-        coded[o, 0] = wires.start(code.at[o - 1, 0], got.at[o - 1, 0], peer[o])
+        code[o - 1, 1] = encode(whole[1], inverse)
     for o in (2, 1, 3):
         coded[o, 1] = wires.start(code.at[o - 1, 1], got.at[o - 1, 1], peer[o])
+    swap[0].wait_recv()
+    total[...] = part[chunk(0, core)] + sibling[0]
     for o in (1, 3, 2):
         scaled[o].wait_recv()
     wires.send = send3

time: 83.8 us -> 83.8 us (level)
  no operation moved by 1% of the time
where the time goes in v9:
time: 83.8 us; the launch traced here: 83.6 us
  Pallas kernels  80.2 us (96%)
  between operations  1.93 us (2%)
  local copies, waits for them, and re-layouts  1.33 us (2%)
    pallas_call x1, Pallas kernels, orthonormalize(): pl.pallas_call(functools.partial(basis_kernel, root), out_shape=[jax.Shap...  35.7 us
    pallas_call x1, Pallas kernels, sum_image(): pl.pallas_call(image_kernel, out_shape=jax.ShapeDtypeStruct((blocks, dept...  21.8 us
    pallas_call x1, Pallas kernels, gather(): pl.pallas_call(gather_kernel, out_shape=[jax.ShapeDtypeStruct((2, rows //...  19.8 us
    pallas_call x2, Pallas kernels, products(): pl.pallas_call(functools.partial(products_kernel, transposed), out_shape=...  2.84 us

profile of v9, /device:TPU:1, one launch (start us, length us, event | category | flops | bytes accessed | tf_op | source)
XLA Modules:
  0.0 83.6 jit_solution(17848806779832817124)
XLA Ops:
  1.3 19.8 %shard_map.72 = (bf16[2,4,4,256,128]{4,3,2,1,0:T(8,128)(2,1)S(1)}, bf16[32,256,256]{2,1,0:T(8,128)(2,1)S(1)}, s32[1,1,32]{2,1,0:T(1,128)S(1)}, s32[1,1,32]{2,1,0:T(1,128)S(1)}) custom-call(bf16[16,256,128]{2,1,0:T(8,128)(2,1)} %bitcast.6, bf16[32,256,256]{2,1,0:T(8,128)(2,1)} %bitcast.5, s32[1,1,32]{2,1,0:T(1,128)} %rows.1, s32[1,1,32]{2,1,0:T(1,128)} %cols.1), custom_call_target="tpu_custom_call" | custom-call | tf_op jit(solution)/shard_map/pallas_call | solution.py:154
  21.1 1.4 %shard_map.73.part = f32[16,256,128]{2,1,0:T(8,128)S(1)} custom-call(s32[1,1]{1,0:T(1,128)S(6)} %copy.19.count_ref, s32[1,1,32]{2,1,0:T(1,128)S(1)} %get-tuple-element.19.row_ref, s32[1,1,32]{2,1,0:T(1,128)S(1)} %get-tuple-element.20.col_ref, bf16[32,256,128]{2,1,0:T(8,128)(2,1)S(1)} %bitcast.4, bf16[32,256,256]{2,1,0:T(8,128)(2,1)S(1)} %get-tuple-element.22.tiles), custom_call_target="tpu_custom_call" | custom-call | tf_op jit(solution)/shard_map/pallas_call | solution.py:473
  22.5 21.8 %shard_map.74.panels = bf16[16,128,256]{2,1,0:T(8,128)(2,1)S(1)} custom-call(f32[16,256,128]{2,1,0:T(8,128)S(1)} %shard_map.73.part), custom_call_target="tpu_custom_call" | custom-call | tf_op jit(solution)/shard_map/pallas_call | solution.py:244
  44.3 1.4 %shard_map.75.part = f32[32,128,256]{2,1,0:T(8,128)S(1)} custom-call(s32[1,1]{1,0:T(1,128)S(6)} %copy.19.count_ref, s32[1,1,32]{2,1,0:T(1,128)S(1)} %get-tuple-element.19.row_ref, s32[1,1,32]{2,1,0:T(1,128)S(1)} %get-tuple-element.20.col_ref, bf16[16,128,256]{2,1,0:T(8,128)(2,1)S(1)} %shard_map.74.panels, bf16[32,256,256]{2,1,0:T(8,128)(2,1)S(1)} %get-tuple-element.22.tiles), custom_call_target="tpu_custom_call" | custom-call | tf_op jit(solution)/shard_map/pallas_call | solution.py:473
  45.8 35.7 %shard_map.76 = (f32[512,128]{1,0:T(8,128)S(1)}, f32[128,128]{1,0:T(8,128)S(1)}, f32[1,1]{1,0:T(1,128)}) custom-call(f32[32,128,256]{2,1,0:T(8,128)S(1)} %shard_map.75.part), custom_call_target="tpu_custom_call" | custom-call | tf_op jit(solution)/shard_map/pallas_call | solution.py:554
  82.1 0.2 conditional.1
  82.3 0.7 copy.22
  83.0 0.6 copy.23
